TPU v7x, 512 devices: a whole 4x4x16 slice. The times are simulated.
512 devices in a mesh: mode: 16 (over x_hi, y, core), space: 32 (over x_lo, z).
Axes of the slice: x: 4 (x_hi: 2, x_lo: 2; x = x_hi * 2 + x_lo), y: 4, z: 16, core: 2. Of those that a mesh axis runs over, the one named last changes fastest.
Arguments:
- residual: float32 [32, 2, 512, 128], P('mode', None, 'space'), may hold values from -6 to 6
- solution: float32 [32, 2, 512, 128], P('mode', None, 'space'), may hold values from -6 to 6
- kl_terms: float32 [21, 2, 512, 128], P(None, None, 'space'), may hold values from -2.5 to 4, as said below
- partner: int32 [32, 24], P('mode'), may hold values from 0 to 31
- kl_index: int32 [32, 24], P('mode'), may hold values from 1 to 20
- coefficient: float32 [32, 24], P('mode'), may hold values from -4 to 4
Outputs:
- image: float32 [32, 2, 512, 128], P('mode', None, 'space')
- solution_new: float32 [32, 2, 512, 128], P('mode', None, 'space')
- residual_new: float32 [32, 2, 512, 128], P('mode', None, 'space')
- direction_new: float32 [32, 2, 512, 128], P('mode', None, 'space')
Inputs may be any that keep to these rules, and one draw needn't show every extreme that they name: kl_terms[0] is positive everywhere.
All inputs are finite; a program needn't handle non-finite values.
Results may differ from a plain program's by a relative error of at most 0.00018.
Values sent between devices are 32-bit elements; how exact they have to be, the bound alone decides.
A program may use at most 64 MiB of HBM per device.

v0:
```python
import jax
import jax.numpy as jnp
from jax import lax
from jax.sharding import PartitionSpec as P

EPS = 1e-06


def padded_2(value, sides, width):
    for axis, dim in sides:
        devices, length = (lax.axis_size(axis), value.shape[dim])
        up = [(i, (i + 1) % devices) for i in range(devices - 1)]
        down = [(j, i) for i, j in up]
        last = lax.slice_in_dim(value, length - width, length, axis=dim)
        leading = lax.slice_in_dim(value, 0, width, axis=dim)
        before = lax.ppermute(last, axis, up)
        after = lax.ppermute(leading, axis, down)
        value = jnp.concatenate([before, value, after], axis=dim)
    return value


def diffuse(values, coeffs):
    pad_v = [(0, 0)] * (values.ndim - 3) + [(1, 1), (0, 0), (1, 1)]
    pad_c = [(0, 0)] * (coeffs.ndim - 3) + [(1, 1), (0, 0), (1, 1)]
    full_v = jnp.pad(values, pad_v)
    full_c = jnp.pad(coeffs, pad_c)
    centre_val = full_v[..., 1:-1, 1:-1, 1:-1]
    centre_cof = full_c[..., 1:-1, 1:-1, 1:-1]
    beside_val = [
        full_v[..., 2:, 1:-1, 1:-1],
        full_v[..., :-2, 1:-1, 1:-1],
        full_v[..., 1:-1, 2:, 1:-1],
        full_v[..., 1:-1, :-2, 1:-1],
        full_v[..., 1:-1, 1:-1, 2:],
        full_v[..., 1:-1, 1:-1, :-2],
    ]
    beside_cof = [
        full_c[..., 2:, 1:-1, 1:-1],
        full_c[..., :-2, 1:-1, 1:-1],
        full_c[..., 1:-1, 2:, 1:-1],
        full_c[..., 1:-1, :-2, 1:-1],
        full_c[..., 1:-1, 1:-1, 2:],
        full_c[..., 1:-1, 1:-1, :-2],
    ]
    total = 0.5 * (centre_cof + beside_cof[0]) * (centre_val - beside_val[0])
    for near_v, near_c in zip(beside_val[1:], beside_cof[1:]):
        total = total + 0.5 * (centre_cof + near_c) * (centre_val - near_v)
    return total


def on_device(residual, solution, kl_terms, partner, kl_index, coefficient):
    padded, coef_pad = (
        padded_2(residual, (("space", 2),), 1),
        padded_2(kl_terms, (("space", 2),), 1),
    )
    image_self = diffuse(padded, coef_pad[0])
    all_fields = lax.all_gather(padded, "mode", axis=0, tiled=True)

    def one_row(entries):
        part_row, term_row, weight_row = entries
        fields = all_fields[part_row]
        local_cof = coef_pad[term_row]
        return jnp.sum(weight_row[:, None, None, None] * diffuse(fields, local_cof), axis=0)

    couple = lax.map(one_row, (partner, kl_index, coefficient))
    image = image_self + couple
    norm_old, curve, energy = lax.psum(
        (jnp.sum(residual * residual), jnp.sum(residual * image), jnp.sum(image * image)),
        ("mode", "space"),
    )
    step_size = curve / (energy + EPS)
    solution_new = solution + step_size * residual
    residual_new = residual - step_size * image
    norm_new = lax.psum(jnp.sum(residual_new * residual_new), ("mode", "space"))
    direction_new = residual_new + norm_new / (norm_old + EPS) * residual
    return (image, solution_new, residual_new, direction_new)


def solution(mesh):
    return jax.shard_map(
        on_device,
        mesh=mesh,
        in_specs=(
            P("mode", None, "space", None),
            P("mode", None, "space", None),
            P(None, None, "space", None),
            P("mode", None),
            P("mode", None),
            P("mode", None),
        ),
        out_specs=(
            P("mode", None, "space", None),
            P("mode", None, "space", None),
            P("mode", None, "space", None),
            P("mode", None, "space", None),
        ),
        check_vma=False,
    )
```

profile of v0, /device:TPU:1, one launch (start us, length us, event | category | flops | bytes accessed | tf_op | source)
XLA Modules:
  0.0 260.2 jit_solution(7887017020321080102)
XLA Ops:
  0.6 0.7 fusion.62
  1.4 4.4 %collective-permute-start.2 = (f32[2,2,1,128]{3,2,1,0:T(1,128)S(1)}, f32[2,2,1,128]{3,2,1,0:T(1,128)S(1)}, u32[]{:S(2)}, u32[]{:S(2)}) collective-permute-start(f32[2,2,1,128]{3,2,1,0:T(1,128)S(1)} %get-tuple-element.142), channel_id=1, source_target_pairs={{0,1},{1,2},{2,3},{3,4},{4,5},{5,6},{6,7},{7,8},{8,9},{9,10},{10,1... | collective-permute-start | bytes 6152 | tf_op jit(solution)/shard_map/ppermute | solution.py:16
  5.7 1.3 collective-permute-start.3
  7.0 1.0 fusion.61
  8.1 4.2 %collective-permute-start = (f32[21,2,1,128]{3,2,1,0:T(1,128)S(1)}, f32[21,2,1,128]{3,2,1,0:T(1,128)S(1)}, u32[]{:S(2)}, u32[]{:S(2)}) collective-permute-start(f32[21,2,1,128]{3,2,1,0:T(1,128)S(1)} %get-tuple-element.138), channel_id=1, source_target_pairs={{0,1},{1,2},{2,3},{3,4},{4,5},{5,6},{6,7},{7,8},{8,9},{9,10},{10,1... | collective-permute-start | bytes 64520 | tf_op jit(solution)/shard_map/ppermute | solution.py:16
  12.3 1.3 collective-permute-start.1
  13.6 0.0 collective-permute-done.2
  13.6 0.0 collective-permute-done.3
  13.6 0.8 pad_maximum_fusion.1
  14.4 27.2 %all_gather.3 = f32[32,2,18,128]{3,1,2,0:T(2,128)S(1)} all-gather(f32[2,2,18,128]{3,1,2,0:T(2,128)S(1)} %copy.38), channel_id=1, replica_groups=mesh['mode'=16,'space'=32] {'mode'}, dimensions={0}, use_global_device_ids=true | all-gather | bytes 626688 | tf_op jit(solution)/shard_map/all_gather | solution.py:57
  41.6 0.0 copy-start.1
  41.6 0.1 copy.39
  41.7 0.0 copy-start.5
  41.7 0.0 copy-start.6
  41.7 0.0 copy-start.7
  41.7 0.0 collective-permute-done
  41.7 0.0 collective-permute-done.1
  41.7 0.8 copy-done.1
  42.6 0.1 pad_maximum_fusion
  42.7 0.0 copy-done.5
  42.7 0.0 copy-done.6
  42.7 0.0 copy-done.7
  42.7 0.0 copy-start
  42.7 0.0 copy-start.4
  42.7 3.9 %while.12 = (s32[]{:T(128)}, f32[2,2,16,128]{3,2,1,0:T(8,128)S(1)}, f32[2,24]{1,0:T(2,128)S(1)}, s32[2,24]{1,0:T(2,128)S(1)}, f32[21,2,18,128]{3,2,1,0:T(8,128)S...) while((s32[]{:T(128)}, f32[2,2,16,128]{3,2,1,0:T(8,128)S(1)}, ...), condition=%wide.region_2.3_spmd, body=%wide.region_0.2_spmd.sunk | while | flops 3045522 | bytes 5367329 | solution.py:65
  42.8 0.6 gather_fusion
  43.4 0.6 gather_fusion.1
  44.0 0.7 fusion.68
  44.7 0.6 gather_fusion
  45.3 0.6 gather_fusion.1
  45.9 0.7 fusion.68
  46.6 0.1 fusion.51
  46.7 0.0 copy-done
  46.7 0.7 multiply_reduce_fusion
  47.4 0.0 copy-start.2
  47.4 108.1 %all-reduce.5 = (f32[]{:T(128)}, f32[]{:T(128)}) all-reduce(f32[]{:T(128)} %get-tuple-element.113, f32[]{:T(128)} %get-tuple-element.114), channel_id=1, replica_groups=mesh['mode'=16,'space'=32] {'mode','space'}, use_global_device_ids=true, to_apply=%region_4.5 | all-reduce | flops 2 | bytes 16 | tf_op jit(solution)/shard_map/psum | solution.py:67
  156.9 0.6 multiply_reduce_fusion.1
  157.5 0.0 copy-start.3
  157.5 100.8 %all-reduce.4 = (f32[]{:T(128)}, f32[]{:T(128)}) all-reduce(f32[]{:T(128)} %get-tuple-element.133, f32[]{:T(128)} %get-tuple-element.112), channel_id=1, replica_groups=mesh['mode'=16,'space'=32] {'mode','space'}, use_global_device_ids=true, to_apply=%region_8.9 | all-reduce | flops 2 | bytes 16 | tf_op jit(solution)/shard_map/psum | solution.py:74
  259.5 0.0 copy-done.4
  259.5 0.6 multiply_add_fusion
  260.2 0.0 copy-done.2
  260.2 0.0 copy-done.3
  (13 shorter events, 0.1 us)
Async XLA Ops:
  1.4 12.2 %collective-permute-start.2 = (f32[2,2,1,128]{3,2,1,0:T(1,128)S(1)}, f32[2,2,1,128]{3,2,1,0:T(1,128)S(1)}, u32[]{:S(2)}, u32[]{:S(2)}) collective-permute-start(f32[2,2,1,128]{3,2,1,0:T(1,128)S(1)} %get-tuple-element.142), channel_id=1, source_target_pairs={{0,1},{1,2},{2,3},{3,4},{4,5},{5,6},{6,7},{7,8},{8,9},{9,10},{10,1... | collective-permute-start | bytes 6152 | tf_op jit(solution)/shard_map/ppermute | solution.py:16
  5.7 7.8 %collective-permute-start.3 = (f32[2,2,1,128]{3,2,1,0:T(1,128)S(1)}, f32[2,2,1,128]{3,2,1,0:T(1,128)S(1)}, u32[]{:S(2)}, u32[]{:S(2)}) collective-permute-start(f32[2,2,1,128]{3,2,1,0:T(1,128)S(1)} %get-tuple-element.143), channel_id=1, source_target_pairs={{1,0},{2,1},{3,2},{4,3},{5,4},{6,5},{7,6},{8,7},{9,8},{10,9},{11,1... | collective-permute-start | bytes 6152 | tf_op jit(solution)/shard_map/ppermute | solution.py:17
  8.1 33.6 %collective-permute-start = (f32[21,2,1,128]{3,2,1,0:T(1,128)S(1)}, f32[21,2,1,128]{3,2,1,0:T(1,128)S(1)}, u32[]{:S(2)}, u32[]{:S(2)}) collective-permute-start(f32[21,2,1,128]{3,2,1,0:T(1,128)S(1)} %get-tuple-element.138), channel_id=1, source_target_pairs={{0,1},{1,2},{2,3},{3,4},{4,5},{5,6},{6,7},{7,8},{8,9},{9,10},{10,1... | collective-permute-start | bytes 64520 | tf_op jit(solution)/shard_map/ppermute | solution.py:16
  12.3 29.4 %collective-permute-start.1 = (f32[21,2,1,128]{3,2,1,0:T(1,128)S(1)}, f32[21,2,1,128]{3,2,1,0:T(1,128)S(1)}, u32[]{:S(2)}, u32[]{:S(2)}) collective-permute-start(f32[21,2,1,128]{3,2,1,0:T(1,128)S(1)} %get-tuple-element.139), channel_id=1, source_target_pairs={{1,0},{2,1},{3,2},{4,3},{5,4},{6,5},{7,6},{8,7},{9,8},{10,9},{11,1... | collective-permute-start | bytes 64520 | tf_op jit(solution)/shard_map/ppermute | solution.py:17
  41.6 1.0 copy-start.1
  41.7 1.0 copy-start.5
  41.7 1.0 copy-start.6
  41.7 1.0 copy-start.7
  42.7 4.0 %copy-start = (f32[2,2,16,128]{3,2,1,0:T(8,128)S(1)}, f32[2,2,16,128]{3,2,1,0:T(8,128)}, u32[]{:S(2)}) copy-start(f32[2,2,16,128]{3,2,1,0:T(8,128)} %param.8) | copy-start | bytes 98308
  42.7 216.8 %copy-start.4 = (f32[2,2,16,128]{3,2,1,0:T(8,128)S(1)}, f32[2,2,16,128]{3,2,1,0:T(8,128)}, u32[]{:S(2)}) copy-start(f32[2,2,16,128]{3,2,1,0:T(8,128)} %param.9) | copy-start | bytes 98308
  47.4 212.8 %copy-start.2 = (f32[2,2,16,128]{3,2,1,0:T(8,128)}, f32[2,2,16,128]{3,2,1,0:T(8,128)S(1)}, u32[]{:S(2)}) copy-start(f32[2,2,16,128]{3,2,1,0:T(8,128)S(1)} %get-tuple-element.135) | copy-start | bytes 98308
  157.5 102.7 %copy-start.3 = (f32[2,2,16,128]{3,2,1,0:T(8,128)}, f32[2,2,16,128]{3,2,1,0:T(8,128)S(1)}, u32[]{:S(2)}) copy-start(f32[2,2,16,128]{3,2,1,0:T(8,128)S(1)} %get-tuple-element.134) | copy-start | bytes 98308
where the time goes:
time: 261 us; the launch traced here: 260 us
  blocking collectives  236 us (90%)
  starting transfers between devices  11.1 us (4%)
  local copies, waits for them, and re-layouts  5.14 us (2%)
  other arithmetic  4.25 us (2%)
  between operations  3.44 us (1%)
    psum x1, blocking collectives, on_device(): lax.psum((jnp.sum(residual * residual), jnp.sum(residual * image), jnp.su...  108 us
    psum x1, blocking collectives, on_device(): norm_new = lax.psum(jnp.sum(residual_new * residual_new), ('mode', 'space'))  101 us
    all_gather x1, blocking collectives, on_device(): all_fields = lax.all_gather(padded, 'mode', axis=0, tiled=True)  27.2 us
    ppermute x2, starting transfers between devices, padded_2(): before = lax.ppermute(last, axis, up)  8.53 us
  transfers between devices with their start and end apart: 4, of which 0 were waited for; matrix products, arithmetic and copies ran while one was open for 1% of the time, Pallas kernels for 0%

commit v1 on v0

v1 whole, which is shorter than its diff:
```python
import jax
import jax.numpy as jnp
from jax import lax
from jax.experimental import pallas as pl
from jax.experimental.pallas import tpu as pltpu
from jax.sharding import PartitionSpec as P

EPS = 1e-6
MESH = pl.DeviceIdType.MESH
KL, TERMS, MODES = 21, 24, 32
F32 = jnp.float32


def group_shift(t, sign=1):
    m, s = lax.axis_index("mode"), lax.axis_index("space")
    xh = (m // 8 + 1 - t // 8) % 2
    y = (m // 2 + sign * ((t // 2 + 1) % 4) + 4) % 4
    c = (m + 1 - t % 2) % 2
    return xh * 8 + y * 2 + c, s


def half_shift(t, sign=1):
    m, s = lax.axis_index("mode"), lax.axis_index("space")
    y = (m // 2 + sign * ((t // 2 + 1) % 4) + 4) % 4
    c = (m + 1 - t % 2) % 2
    return (m // 8) * 8 + y * 2 + c, s


def plane_shift(t):
    m, s = lax.axis_index("mode"), lax.axis_index("space")
    x = ((m // 8) * 2 + s // 16 + t // 8 + 1) % 4
    y = (m // 2 + t // 2 + 1) % 4
    c = (m + 1 - t % 2) % 2
    return (x // 2) * 8 + y * 2 + c, (x % 2) * 16 + s % 16


def z_shift(t):
    m, s = lax.axis_index("mode"), lax.axis_index("space")
    return m, (s // 16) * 16 + (s + jnp.where(t < 8, 8 - t, t + 1)) % 16


def loop(n, body):
    def step(t, carry):
        body(t)
        return carry

    lax.fori_loop(0, n, step, 0)


def galerkin(
    res_hbm, kl_hbm, part_hbm, term_hbm, coef_hbm,
    image_ref, sums_ref,
    res, klv, part_v, term_v, coef_v,
    pieces, edges, kl_edge, ints, floats,
    got, got_edges, got_kl, got_ints, got_floats, int_s, float_s,
    cof, aa, ff, img, back, sum_a, sums_a, sum_b, sums_b,
    in_sem, main_ss, main_rs, edge_ss, edge_rs, kle_ss, kle_rs,
    int_ss, int_rs, flo_ss, flo_rs, smem_sem,
    a_ss, a_rs, b_ss, b_rs, back_ss, back_rs,
):
    m, s = lax.axis_index("mode"), lax.axis_index("space")
    g, q = m // 8, m % 8
    own_plane = ((m // 8) * 2 + s // 16) * 8 + m % 8
    z_at = s % 16
    low, high = s > 0, s < 31
    first, last = q == 0, q == 7
    get_low, get_high = first & low, last & high
    get_edge = get_low | get_high
    put_kl = (first & high) | (last & low)

    loads = [
        pltpu.make_async_copy(a, b, in_sem.at[i])
        for i, (a, b) in enumerate(
            (
                (res_hbm, res.at[:, :, 8:24, :]),
                (part_hbm, part_v),
                (term_hbm, term_v),
                (coef_hbm, coef_v),
                (kl_hbm, klv.at[:, :, 8:24, :]),
            )
        )
    ]
    for load in loads:
        load.start()

    barrier = pltpu.get_barrier_semaphore()

    def greet(device):
        pl.semaphore_signal(barrier, inc=1, device_id=device, device_id_type=MESH)

    loop(15, lambda t: greet(z_shift(t)))
    loop(31, lambda t: greet(plane_shift(t)))

    @pl.when(get_low)
    def _():
        loop(16, lambda t: greet((t, jnp.maximum(s - 1, 0))))

    @pl.when(get_high)
    def _():
        loop(16, lambda t: greet((t, jnp.minimum(s + 1, 31))))

    for load in loads[:4]:
        load.wait()
    for i in range(2):
        for z in range(2):
            res[i, z, 0:8, :] = jnp.zeros((8, 128), F32)
            res[i, z, 24:32, :] = jnp.zeros((8, 128), F32)
    for j in range(8):
        for i in range(2):
            for z in range(2):
                pieces[j, i, 4 * z : 4 * z + 4, :] = res[i, z, 2 * j + 7 : 2 * j + 11, :]
    for i in range(2):
        for z in range(2):
            edges[0, 2 * i + z : 2 * i + z + 1, :] = res[i, z, 23:24, :]
            edges[1, 2 * i + z : 2 * i + z + 1, :] = res[i, z, 8:9, :]
    ints[0, :, 0:TERMS] = part_v[...]
    ints[1, :, 0:TERMS] = term_v[...]
    floats[:, 0:TERMS] = coef_v[...]
    loads[4].wait()
    end = jnp.where(first, 23, 8)
    for z in range(2):
        kl_edge[:, z : z + 1, :] = klv[:, z, pl.ds(end, 1), :]

    pl.semaphore_wait(barrier, 46 + 2 * low.astype(jnp.int32) + 2 * high.astype(jnp.int32))

    def main_copy(t):
        to = group_shift(t)
        return pltpu.make_async_remote_copy(
            src_ref=pieces.at[to[0] % 8], dst_ref=got.at[m], send_sem=main_ss.at[t], recv_sem=main_rs.at[t],
            device_id=to, device_id_type=MESH,
        )

    def edge_copy(up, half):
        to = (half * 8, jnp.minimum(s + 1, 31)) if up else (half * 8 + 7, jnp.maximum(s - 1, 0))
        return pltpu.make_async_remote_copy(
            src_ref=edges.at[0 if up else 1], dst_ref=got_edges.at[m], send_sem=edge_ss.at[(0 if up else 2) + half],
            recv_sem=edge_rs.at[m], device_id=to, device_id_type=MESH,
        )

    def kl_copy():
        return pltpu.make_async_remote_copy(
            src_ref=kl_edge, dst_ref=got_kl, send_sem=kle_ss, recv_sem=kle_rs,
            device_id=(m, jnp.where(first, jnp.minimum(s + 1, 31), jnp.maximum(s - 1, 0))), device_id_type=MESH,
        )

    def int_copy(t):
        return pltpu.make_async_remote_copy(
            src_ref=ints, dst_ref=got_ints.at[q], send_sem=int_ss.at[t], recv_sem=int_rs.at[t],
            device_id=half_shift(t), device_id_type=MESH,
        )

    def float_copy(t):
        return pltpu.make_async_remote_copy(
            src_ref=floats, dst_ref=got_floats.at[q], send_sem=flo_ss.at[t], recv_sem=flo_rs.at[t],
            device_id=half_shift(t), device_id_type=MESH,
        )

    @pl.when(put_kl)
    def _():
        kl_copy().start()

    @pl.when(high)
    def _():
        edge_copy(True, 0).start()
        edge_copy(True, 1).start()

    @pl.when(low)
    def _():
        edge_copy(False, 0).start()
        edge_copy(False, 1).start()

    loop(15, lambda t: main_copy(t).start())

    def start_tables(t):
        int_copy(t).start()
        float_copy(t).start()

    loop(7, start_tables)

    got[m] = pieces[q]
    got_ints[q] = ints[...]
    got_floats[q] = floats[...]

    for z in range(2):
        for r in range(4):
            cof[:, 4 * z + r : 4 * z + r + 1, :] = klv[:, z, pl.ds(2 * q + 7 + r, 1), :]

    @pl.when(first)
    def _():
        cof[:, 0:1, :] = jnp.zeros((KL, 1, 128), F32)
        cof[:, 4:5, :] = jnp.zeros((KL, 1, 128), F32)

    @pl.when(last)
    def _():
        cof[:, 3:4, :] = jnp.zeros((KL, 1, 128), F32)
        cof[:, 7:8, :] = jnp.zeros((KL, 1, 128), F32)

    @pl.when(get_edge)
    def _():
        kl_copy().wait_recv()

    @pl.when(get_low)
    def _():
        cof[:, 0:1, :] = got_kl[:, 0:1, :]
        cof[:, 4:5, :] = got_kl[:, 1:2, :]

    @pl.when(get_high)
    def _():
        cof[:, 3:4, :] = got_kl[:, 0:1, :]
        cof[:, 7:8, :] = got_kl[:, 1:2, :]

    lane = lax.broadcasted_iota(jnp.int32, (8, 128), 1)
    sub = lax.broadcasted_iota(jnp.int32, (8, 128), 0)
    inner = jnp.where(lane < 127, 0.5, 0.0).astype(F32)
    border = (0.5 + jnp.where(lane == 0, 0.5, 0.0) + jnp.where(lane == 127, 0.5, 0.0)).astype(F32)
    valid = (sub % 4 == 1) | (sub % 4 == 2)

    def coefficients(k):
        a = cof[k]
        aa[k, 0] = 0.5 * (a + pltpu.roll(a, 7, 0))
        aa[k, 1] = inner * (a + pltpu.roll(a, 127, 1))
        aa[k, 2] = 0.5 * (a + pltpu.roll(a, 4, 0))
        aa[k, 3] = border * a

    loop(KL, coefficients)

    def take_tables(t):
        int_copy(t).wait_recv()
        float_copy(t).wait_recv()

    loop(7, take_tables)
    to_smem = [
        pltpu.make_async_copy(got_ints, int_s, smem_sem.at[0]),
        pltpu.make_async_copy(got_floats, float_s, smem_sem.at[1]),
    ]
    for copy in to_smem:
        copy.start()

    loop(15, lambda t: main_copy(t).wait_recv())

    @pl.when(get_edge)
    def _():
        def take_edge(t):
            pltpu.make_async_remote_copy(
                src_ref=edges.at[0], dst_ref=got_edges.at[t], send_sem=edge_ss.at[0], recv_sem=edge_rs.at[t],
                device_id=(m, s), device_id_type=MESH,
            ).wait_recv()

        loop(16, take_edge)

    @pl.when(get_low)
    def _():
        for i in range(2):
            for z in range(2):
                got[:, i, 4 * z : 4 * z + 1, :] = got_edges[:, 2 * i + z : 2 * i + z + 1, :]

    @pl.when(get_high)
    def _():
        for i in range(2):
            for z in range(2):
                got[:, i, 4 * z + 3 : 4 * z + 4, :] = got_edges[:, 2 * i + z : 2 * i + z + 1, :]

    def differences(d):
        for i in range(2):
            v = got[d, i]
            ff[2 * d + i, 0] = v - pltpu.roll(v, 7, 0)
            ff[2 * d + i, 1] = v - pltpu.roll(v, 127, 1)
            ff[2 * d + i, 2] = v - pltpu.roll(v, 4, 0)
            ff[2 * d + i, 3] = v

    loop(16, differences)
    for copy in to_smem:
        copy.wait()

    def one_mode(n, carry):
        norm, curve, energy = carry
        own = g * 16 + n
        flux_x = aa[0, 0] * ff[own, 0]
        flux_y = aa[0, 1] * ff[own, 1]
        rest = aa[0, 2] * ff[own, 2] + aa[0, 3] * ff[own, 3]
        for e in range(TERMS):
            p = int_s[n // 2, 0, n % 2, e] & 31
            k = int_s[n // 2, 1, n % 2, e] & 31
            w = float_s[n // 2, n % 2, e]
            flux_x += w * (aa[k, 0] * ff[p, 0])
            flux_y += w * (aa[k, 1] * ff[p, 1])
            rest += w * (aa[k, 2] * ff[p, 2] + aa[k, 3] * ff[p, 3])
        out = rest + (flux_x - pltpu.roll(flux_x, 1, 0)) + (flux_y - pltpu.roll(flux_y, 1, 1))
        img[n] = out
        out = jnp.where(valid, out, 0.0)
        v = jnp.where(valid, ff[own, 3], 0.0)
        return norm + v * v, curve + v * out, energy + out * out

    zero = jnp.zeros((8, 128), F32)
    parts = lax.fori_loop(0, 16, one_mode, (zero, zero, zero))

    sum_a[...] = jnp.zeros((4, 128), F32)
    for i in range(3):
        sum_a[i : i + 1, :] = jnp.sum(parts[i], axis=0, keepdims=True)

    def a_copy(t):
        return pltpu.make_async_remote_copy(
            src_ref=sum_a, dst_ref=sums_a.at[own_plane], send_sem=a_ss.at[t], recv_sem=a_rs.at[t],
            device_id=plane_shift(t), device_id_type=MESH,
        )

    def b_copy(t):
        return pltpu.make_async_remote_copy(
            src_ref=sum_b, dst_ref=sums_b.at[z_at], send_sem=b_ss.at[t], recv_sem=b_rs.at[t],
            device_id=z_shift(t), device_id_type=MESH,
        )

    def back_copy(t):
        to = half_shift(t)
        return pltpu.make_async_remote_copy(
            src_ref=img.at[pl.ds(2 * (to[0] % 8), 2)], dst_ref=back.at[q], send_sem=back_ss.at[t], recv_sem=back_rs.at[t],
            device_id=to, device_id_type=MESH,
        )

    loop(31, lambda t: a_copy(t).start())
    sums_a[own_plane] = sum_a[...]
    loop(31, lambda t: a_copy(t).wait_recv())
    sum_b[...] = jnp.sum(sums_a[...], axis=0)
    loop(15, lambda t: b_copy(t).start())
    loop(7, lambda t: back_copy(t).start())
    sums_b[z_at] = sum_b[...]
    back[q] = img[pl.ds(2 * q, 2)]

    loop(7, lambda t: back_copy(t).wait_recv())
    for i in range(2):
        for z in range(2):
            for h in range(2):
                tile = pltpu.roll(back[4 * h, i], 7 - 4 * z, 0)
                for j in range(1, 4):
                    tile = jnp.where(sub // 2 == j, pltpu.roll(back[4 * h + j, i], (2 * j + 7 - 4 * z) % 8, 0), tile)
                image_ref[i, z, 8 * h : 8 * h + 8, :] = tile

    loop(15, lambda t: main_copy(t).wait_send())

    def tables_left(t):
        int_copy(t).wait_send()
        float_copy(t).wait_send()
        back_copy(t).wait_send()

    loop(7, tables_left)
    loop(31, lambda t: a_copy(t).wait_send())

    @pl.when(put_kl)
    def _():
        kl_copy().wait_send()

    @pl.when(high)
    def _():
        edge_copy(True, 0).wait_send()
        edge_copy(True, 1).wait_send()

    @pl.when(low)
    def _():
        edge_copy(False, 0).wait_send()
        edge_copy(False, 1).wait_send()

    loop(15, lambda t: b_copy(t).wait_recv())
    sums_ref[...] = jnp.sum(sums_b[...], axis=0)
    loop(15, lambda t: b_copy(t).wait_send())


def update(image_in, sums_ref, res_ref, sol_ref, image_ref, sol_out, res_out, dir_out):
    sums = jnp.sum(sums_ref[...], axis=1, keepdims=True)
    norm, curve, energy = sums[0:1], sums[1:2], sums[2:3]
    step = curve / (energy + EPS)
    norm_new = jnp.maximum(norm - 2.0 * step * curve + step * step * energy, 0.0)
    beta = norm_new / (norm + EPS)
    image = image_in[...].reshape(64, 128)
    r = res_ref[...].reshape(64, 128)
    image_ref[...] = image_in[...]
    sol_out[...] = (sol_ref[...].reshape(64, 128) + step * r).reshape(2, 2, 16, 128)
    r_new = r - step * image
    res_out[...] = r_new.reshape(2, 2, 16, 128)
    dir_out[...] = (r_new + beta * r).reshape(2, 2, 16, 128)


def on_device(residual, solution, kl_terms, partner, kl_index, coefficient):
    vmem = pl.BlockSpec(memory_space=pltpu.VMEM)
    anywhere = pl.BlockSpec(memory_space=pl.ANY)
    dma = pltpu.SemaphoreType.DMA
    field = jax.ShapeDtypeStruct(residual.shape, F32)
    i32 = jnp.int32
    image, sums = pl.pallas_call(
        galerkin,
        out_shape=(field, jax.ShapeDtypeStruct((4, 128), F32)),
        in_specs=[anywhere] * 5,
        out_specs=(vmem, vmem),
        scratch_shapes=[
            pltpu.VMEM((2, 2, 32, 128), F32),
            pltpu.VMEM((KL, 2, 32, 128), F32),
            pltpu.VMEM((2, TERMS), i32),
            pltpu.VMEM((2, TERMS), i32),
            pltpu.VMEM((2, TERMS), F32),
            pltpu.VMEM((8, 2, 8, 128), F32),
            pltpu.VMEM((2, 4, 128), F32),
            pltpu.VMEM((KL, 2, 128), F32),
            pltpu.VMEM((2, 2, 128), i32),
            pltpu.VMEM((2, 128), F32),
            pltpu.VMEM((16, 2, 8, 128), F32),
            pltpu.VMEM((16, 4, 128), F32),
            pltpu.VMEM((KL, 2, 128), F32),
            pltpu.VMEM((8, 2, 2, 128), i32),
            pltpu.VMEM((8, 2, 128), F32),
            pltpu.SMEM((8, 2, 2, 128), i32),
            pltpu.SMEM((8, 2, 128), F32),
            pltpu.VMEM((KL, 8, 128), F32),
            pltpu.VMEM((32, 4, 8, 128), F32),
            pltpu.VMEM((MODES, 4, 8, 128), F32),
            pltpu.VMEM((16, 8, 128), F32),
            pltpu.VMEM((8, 2, 8, 128), F32),
            pltpu.VMEM((4, 128), F32),
            pltpu.VMEM((32, 4, 128), F32),
            pltpu.VMEM((4, 128), F32),
            pltpu.VMEM((16, 4, 128), F32),
            dma((5,)),
            dma((15,)), dma((15,)),
            dma((4,)), dma((16,)),
            dma, dma,
            dma((7,)), dma((7,)),
            dma((7,)), dma((7,)),
            dma((2,)),
            dma((31,)), dma((31,)),
            dma((15,)), dma((15,)),
            dma((7,)), dma((7,)),
        ],
        compiler_params=pltpu.CompilerParams(
            collective_id=0, has_side_effects=True, vmem_limit_bytes=60 << 20
        ),
        name="galerkin",
    )(residual, kl_terms, partner, kl_index, coefficient)
    return pl.pallas_call(
        update,
        out_shape=(field, field, field, field),
        in_specs=[vmem] * 4,
        out_specs=(vmem,) * 4,
        compiler_params=pltpu.CompilerParams(vmem_limit_bytes=60 << 20),
        name="update",
    )(image, sums, residual, solution)


def solution(mesh):
    field = P("mode", None, "space", None)
    row = P("mode", None)
    return jax.shard_map(
        on_device,
        mesh=mesh,
        in_specs=(field, field, P(None, None, "space", None), row, row, row),
        out_specs=(field, field, field, field),
        check_vma=False,
    )
```

time: 261 us -> 41.7 us (0.16)
  blocking collectives: 236 us -> 0 us
  Pallas kernels: 0 us -> 40.8 us
  starting transfers between devices: 11.1 us -> 0 us
  local copies, waits for them, and re-layouts: 5.14 us -> 0 us
  other arithmetic: 4.25 us -> 0 us
  between operations: 3.44 us -> 0.64 us
    psum x2 -> x0, blocking collectives: 209 us -> none  [the longest x1 108 us: on_device(): lax.psum((jnp.sum(residual * residual), jnp.sum(residual * image), jnp.su...]
    pallas_call x0 -> x2, Pallas kernels: none -> 40.8 us  [the longest x1 39.3 us: on_device(): pl.pallas_call(galerkin, out_shape=(field, jax.ShapeDtypeStruct((4, 128),...]
    all_gather x1 -> x0, blocking collectives: 27.2 us -> none  [on_device(): all_fields = lax.all_gather(padded, 'mode', axis=0, tiled=True)]
    ppermute x4 -> x0, starting transfers between devices: 11.1 us -> none  [the longest x2 8.53 us: padded_2(): before = lax.ppermute(last, axis, up)]
    reduce_sum x4 -> x0, other arithmetic: 2.64 us -> none  [the longest x2 1.33 us: one_row(): jnp.sum(weight_row[:, None, None, None] * diffuse(fields, local_cof), axi...]
  transfers between devices with their start and end apart: 4 -> 0, of which waited for: 0 -> 0; matrix products, arithmetic and copies ran while one was open for 1% -> 0% of each run, Pallas kernels for 0% -> 0%
where the time goes in v1:
time: 41.7 us; the launch traced here: 41.5 us
  Pallas kernels  40.8 us (98%)
  between operations  0.64 us (2%)
    pallas_call x1, Pallas kernels, on_device(): pl.pallas_call(galerkin, out_shape=(field, jax.ShapeDtypeStruct((4, 128),...  39.3 us
    pallas_call x1, Pallas kernels, on_device(): pl.pallas_call(update, out_shape=(field, field, field, field), in_specs=[...  1.56 us

profile of v1, /device:TPU:1, one launch (start us, length us, event | category | flops | bytes accessed | tf_op | source)
XLA Modules:
  0.0 41.5 jit_solution(13322188231725862548)
XLA Ops:
  0.6 39.3 %galerkin.1 = (f32[2,2,16,128]{3,2,1,0:T(8,128)}, f32[4,128]{1,0:T(4,128)}) custom-call(f32[2,2,16,128]{3,2,1,0:T(8,128)} %res_ref.1, f32[21,2,16,128]{3,2,1,0:T(8,128)} %kl_hbm.1, s32[2,24]{1,0:T(2,128)} %part_hbm.1, s32[2,24]{1,0:T(2,128)} %term_hbm.1, f32[2,24]{1,0:T(2,128)} %coef_hbm.1), custom_call_target="tpu_custom_call" | custom-call | tf_op jit(solution)/shard_map/galerkin/pallas_call | solution.py:388
  39.9 1.6 %update.1 = (f32[2,2,16,128]{3,2,1,0:T(8,128)}, f32[2,2,16,128]{3,2,1,0:T(8,128)}, f32[2,2,16,128]{3,2,1,0:T(8,128)}, f32[2,2,16,128]{3,2,1,0:T(8,128)}) custom-call(f32[2,2,16,128]{3,2,1,0:T(8,128)} %get-tuple-element.6.image_in, f32[4,128]{1,0:T(4,128)} %get-tuple-element.7.sums_ref, f32[2,2,16,128]{3,2,1,0:T(8,128)} %res_ref.1, f32[2,2,16,128]{3,2,1,0:T(8,128)} %sol_ref.1), custom_call_target="tpu_custom_call" | custom-call | tf_op jit(solution)/shard_map/update/pallas_call | solution.py:436

commit v2 on v1

--- a/solution.py
+++ b/solution.py
@@ -39,6 +39,11 @@
     return m, (s // 16) * 16 + (s + jnp.where(t < 8, 8 - t, t + 1)) % 16
 
 
+def along_z(d):
+    m, s = lax.axis_index("mode"), lax.axis_index("space")
+    return m, (s // 16) * 16 + (s + d + 16) % 16
+
+
 def loop(n, body):
     def step(t, carry):
         body(t)
@@ -48,15 +53,15 @@
 
 
 def galerkin(
-    res_hbm, kl_hbm, part_hbm, term_hbm, coef_hbm,
-    image_ref, sums_ref,
-    res, klv, part_v, term_v, coef_v,
+    res_hbm, sol_hbm, kl_hbm, part_hbm, term_hbm, coef_hbm,
+    image_ref, sol_ref, res_ref, dir_ref,
+    res, sol, klv, part_v, term_v, coef_v,
     pieces, edges, kl_edge, ints, floats,
     got, got_edges, got_kl, got_ints, got_floats, int_s, float_s,
     cof, aa, ff, img, back, sum_a, sums_a, sum_b, sums_b,
     in_sem, main_ss, main_rs, edge_ss, edge_rs, kle_ss, kle_rs,
     int_ss, int_rs, flo_ss, flo_rs, smem_sem,
-    a_ss, a_rs, b_ss, b_rs, back_ss, back_rs,
+    a_ss, a_rs, b_ss, b_rs, back_ss, back_rs, ring_sem,
 ):
     m, s = lax.axis_index("mode"), lax.axis_index("space")
     g, q = m // 8, m % 8
@@ -77,6 +82,7 @@
                 (term_hbm, term_v),
                 (coef_hbm, coef_v),
                 (kl_hbm, klv.at[:, :, 8:24, :]),
+                (sol_hbm, sol),
             )
         )
     ]
@@ -88,7 +94,8 @@
     def greet(device):
         pl.semaphore_signal(barrier, inc=1, device_id=device, device_id_type=MESH)
 
-    loop(15, lambda t: greet(z_shift(t)))
+    greet(along_z(1))
+    greet(along_z(-1))
     loop(31, lambda t: greet(plane_shift(t)))
 
     @pl.when(get_low)
@@ -121,7 +128,16 @@
     for z in range(2):
         kl_edge[:, z : z + 1, :] = klv[:, z, pl.ds(end, 1), :]
 
-    pl.semaphore_wait(barrier, 46 + 2 * low.astype(jnp.int32) + 2 * high.astype(jnp.int32))
+    pl.semaphore_wait(barrier, 33 + 2 * low.astype(jnp.int32) + 2 * high.astype(jnp.int32))
+
+    def tell(i):
+        for d in (1 << i, -(1 << i)):
+            pl.semaphore_signal(ring_sem.at[i], inc=1, device_id=along_z(d), device_id_type=MESH)
+
+    def hear(i):
+        pl.semaphore_wait(ring_sem.at[i], 2)
+
+    tell(0)
 
     def main_copy(t):
         to = group_shift(t)
@@ -177,6 +193,8 @@
 
     loop(7, start_tables)
 
+    hear(0)
+    tell(1)
     got[m] = pieces[q]
     got_ints[q] = ints[...]
     got_floats[q] = floats[...]
@@ -223,6 +241,9 @@
         aa[k, 3] = border * a
 
     loop(KL, coefficients)
+
+    hear(1)
+    tell(2)
 
     def take_tables(t):
         int_copy(t).wait_recv()
@@ -321,6 +342,7 @@
     sums_a[own_plane] = sum_a[...]
     loop(31, lambda t: a_copy(t).wait_recv())
     sum_b[...] = jnp.sum(sums_a[...], axis=0)
+    hear(2)
     loop(15, lambda t: b_copy(t).start())
     loop(7, lambda t: back_copy(t).start())
     sums_b[z_at] = sum_b[...]
@@ -359,39 +381,49 @@
         edge_copy(False, 0).wait_send()
         edge_copy(False, 1).wait_send()
 
+    loads[5].wait()
+
     loop(15, lambda t: b_copy(t).wait_recv())
-    sums_ref[...] = jnp.sum(sums_b[...], axis=0)
-    loop(15, lambda t: b_copy(t).wait_send())
-
-
-def update(image_in, sums_ref, res_ref, sol_ref, image_ref, sol_out, res_out, dir_out):
-    sums = jnp.sum(sums_ref[...], axis=1, keepdims=True)
+    sums = jnp.sum(jnp.sum(sums_b[...], axis=0), axis=1, keepdims=True)
     norm, curve, energy = sums[0:1], sums[1:2], sums[2:3]
     step = curve / (energy + EPS)
     norm_new = jnp.maximum(norm - 2.0 * step * curve + step * step * energy, 0.0)
     beta = norm_new / (norm + EPS)
-    image = image_in[...].reshape(64, 128)
-    r = res_ref[...].reshape(64, 128)
-    image_ref[...] = image_in[...]
-    sol_out[...] = (sol_ref[...].reshape(64, 128) + step * r).reshape(2, 2, 16, 128)
-    r_new = r - step * image
-    res_out[...] = r_new.reshape(2, 2, 16, 128)
-    dir_out[...] = (r_new + beta * r).reshape(2, 2, 16, 128)
+    for i in range(2):
+        for z in range(2):
+            for h in range(2):
+                rows = pl.ds(8 * h, 8)
+                r = res[i, z, 8 + 8 * h : 16 + 8 * h, :]
+                sol_ref[i, z, rows, :] = sol[i, z, rows, :] + step * r
+                r_new = r - step * image_ref[i, z, rows, :]
+                res_ref[i, z, rows, :] = r_new
+                dir_ref[i, z, rows, :] = r_new + beta * r
+    loop(15, lambda t: b_copy(t).wait_send())
+
+
+def deliver(*refs):
+    sem = refs[8]
+    copies = [pltpu.make_async_copy(refs[i], refs[4 + i], sem.at[i]) for i in range(4)]
+    for copy in copies:
+        copy.start()
+    for copy in copies:
+        copy.wait()
 
 
 def on_device(residual, solution, kl_terms, partner, kl_index, coefficient):
     vmem = pl.BlockSpec(memory_space=pltpu.VMEM)
     anywhere = pl.BlockSpec(memory_space=pl.ANY)
     dma = pltpu.SemaphoreType.DMA
-    field = jax.ShapeDtypeStruct(residual.shape, F32)
+    field = pltpu.VMEM(residual.shape, F32)
     i32 = jnp.int32
-    image, sums = pl.pallas_call(
+    results = pl.pallas_call(
         galerkin,
-        out_shape=(field, jax.ShapeDtypeStruct((4, 128), F32)),
-        in_specs=[anywhere] * 5,
-        out_specs=(vmem, vmem),
+        out_shape=(field,) * 4,
+        in_specs=[anywhere] * 6,
+        out_specs=(vmem,) * 4,
         scratch_shapes=[
             pltpu.VMEM((2, 2, 32, 128), F32),
+            pltpu.VMEM((2, 2, 16, 128), F32),
             pltpu.VMEM((KL, 2, 32, 128), F32),
             pltpu.VMEM((2, TERMS), i32),
             pltpu.VMEM((2, TERMS), i32),
@@ -417,7 +449,7 @@
             pltpu.VMEM((32, 4, 128), F32),
             pltpu.VMEM((4, 128), F32),
             pltpu.VMEM((16, 4, 128), F32),
-            dma((5,)),
+            dma((6,)),
             dma((15,)), dma((15,)),
             dma((4,)), dma((16,)),
             dma, dma,
@@ -427,20 +459,22 @@
             dma((31,)), dma((31,)),
             dma((15,)), dma((15,)),
             dma((7,)), dma((7,)),
+            pltpu.SemaphoreType.REGULAR((3,)),
         ],
         compiler_params=pltpu.CompilerParams(
             collective_id=0, has_side_effects=True, vmem_limit_bytes=60 << 20
         ),
         name="galerkin",
-    )(residual, kl_terms, partner, kl_index, coefficient)
+    )(residual, solution, kl_terms, partner, kl_index, coefficient)
     return pl.pallas_call(
-        update,
-        out_shape=(field, field, field, field),
+        deliver,
+        out_shape=(jax.ShapeDtypeStruct(residual.shape, F32),) * 4,
         in_specs=[vmem] * 4,
-        out_specs=(vmem,) * 4,
+        out_specs=(anywhere,) * 4,
+        scratch_shapes=[dma((4,))],
         compiler_params=pltpu.CompilerParams(vmem_limit_bytes=60 << 20),
-        name="update",
-    )(image, sums, residual, solution)
+        name="deliver",
+    )(*(pltpu.with_memory_space_constraint(a, pltpu.VMEM) for a in results))
 
 
 def solution(mesh):

time: 41.7 us -> 40 us (0.959)
  Pallas kernels: 40.8 us -> 39.3 us
    pallas_call x2, Pallas kernels: 40.8 us -> 39.3 us  [the longest x1 38.6 us: on_device(): pl.pallas_call(galerkin, out_shape=(field,) * 4, in_specs=[anywhere] * 6,...]
where the time goes in v2:
time: 40 us; the launch traced here: 39.9 us
  Pallas kernels  39.3 us (98%)
  between operations  0.64 us (2%)
    pallas_call x1, Pallas kernels, on_device(): pl.pallas_call(galerkin, out_shape=(field,) * 4, in_specs=[anywhere] * 6,...  38.6 us

profile of v2, /device:TPU:1, one launch (start us, length us, event | category | flops | bytes accessed | tf_op | source)
XLA Modules:
  0.0 39.9 jit_solution(8234323132990022125)
XLA Ops:
  0.6 38.6 %galerkin.1 = (f32[2,2,16,128]{3,2,1,0:T(8,128)S(1)}, f32[2,2,16,128]{3,2,1,0:T(8,128)S(1)}, f32[2,2,16,128]{3,2,1,0:T(8,128)S(1)}, f32[2,2,16,128]{3,2,1,0:T(8,128)S(1)}) custom-call(f32[2,2,16,128]{3,2,1,0:T(8,128)} %res_hbm.1, f32[2,2,16,128]{3,2,1,0:T(8,128)} %sol_hbm.1, f32[21,2,16,128]{3,2,1,0:T(8,128)} %kl_hbm.1, s32[2,24]{1,0:T(2,128)} %part_hbm.1, ...), custom_call_target="tpu_custom_call" | custom-call | tf_op jit(solution)/shard_map/galerkin/pallas_call | solution.py:419
  39.2 0.7 %deliver.1 = (f32[2,2,16,128]{3,2,1,0:T(8,128)}, f32[2,2,16,128]{3,2,1,0:T(8,128)}, f32[2,2,16,128]{3,2,1,0:T(8,128)}, f32[2,2,16,128]{3,2,1,0:T(8,128)}) custom-call(f32[2,2,16,128]{3,2,1,0:T(8,128)S(1)} %get-tuple-element.8.refs_0_, f32[2,2,16,128]{3,2,1,0:T(8,128)S(1)} %get-tuple-element.9.refs_1_, f32[2,2,16,128]{3,2,1,0:T(8,128)S(1)} %get-tuple-element.10.refs_2_, ...), custom_call_target="tpu_custom_call" | custom-call | tf_op jit(solution)/shard_map/deliver/pallas_call | solution.py:469

commit v3 on v2

v3 whole, which is shorter than its diff:
```python
import jax
import jax.numpy as jnp
from jax import lax
from jax.experimental import pallas as pl
from jax.experimental.pallas import tpu as pltpu
from jax.sharding import PartitionSpec as P

EPS = 1e-6
MESH = pl.DeviceIdType.MESH
KL, TERMS, MODES = 21, 24, 32
F32 = jnp.float32


def hops(dx, dy):
    return min(dx, 4 - dx) + min(dy, 4 - dy)


GROUP = sorted(((a, b, d) for a in (0, 1) for b in range(4) for d in (0, 1) if a or b or d), key=lambda t: (-hops(2 * t[0], t[1]), -t[2]))
HALF = [t[1:] for t in GROUP if not t[0]]
PLANE = sorted(((a, b, d) for a in range(4) for b in range(4) for d in (0, 1) if a or b or d), key=lambda t: (-hops(t[0], t[1]), -t[2]))
RING = [8, 7, 9, 6, 10, 5, 11, 4, 12, 3, 13, 2, 14, 1, 15]


def galerkin(
    res_hbm, sol_hbm, kl_hbm, part_hbm, term_hbm, coef_hbm,
    image_ref, sol_ref, res_ref, dir_ref,
    res, sol, klv, part_v, term_v, coef_v,
    pieces, edges, kl_edge, ints, floats,
    got, got_edges, got_kl, got_ints, got_floats, int_s, float_s,
    cof, aa, wa, ff, img, back, sum_a, sums_a, sum_b, sums_b,
    in_sem, main_ss, main_rs, edge_ss, edge_rs, kle_ss, kle_rs,
    int_ss, int_rs, flo_ss, flo_rs, smem_sem,
    a_ss, a_rs, b_ss, b_rs, back_ss, back_rs, ring_sem,
):
    m, s = lax.axis_index("mode"), lax.axis_index("space")
    g, q = m // 8, m % 8
    xh, y, c, xl, z_at = g, (m // 2) % 4, m % 2, s // 16, s % 16
    ys = [(y + b) % 4 for b in range(4)]
    cs = [c, 1 - c]
    x_now = xh * 2 + xl
    xs = [(x_now + a) % 4 for a in range(4)]
    row_of = [[ys[b] * 2 + cs[d] for d in range(2)] for b in range(4)]
    half_of = [g * 8, (1 - g) * 8]
    chip_x = [((x // 2) * 8, (x % 2) * 16 + z_at) for x in xs]
    own_plane = x_now * 8 + q
    low, high = s > 0, s < 31
    first, last = q == 0, q == 7
    get_low, get_high = first & low, last & high
    get_edge = get_low | get_high
    put_kl = (first & high) | (last & low)
    below, above = jnp.maximum(s - 1, 0), jnp.minimum(s + 1, 31)

    loads = [
        pltpu.make_async_copy(a, b, in_sem.at[i])
        for i, (a, b) in enumerate(
            (
                (res_hbm, res.at[:, :, 8:24, :]),
                (part_hbm, part_v),
                (term_hbm, term_v),
                (coef_hbm, coef_v),
                (kl_hbm, klv.at[:, :, 8:24, :]),
                (sol_hbm, sol),
            )
        )
    ]
    for load in loads:
        load.start()

    barrier = pltpu.get_barrier_semaphore()

    def greet(device):
        pl.semaphore_signal(barrier, inc=1, device_id=device, device_id_type=MESH)

    def along_z(d):
        return m, xl * 16 + (z_at + d) % 16

    def in_plane(t):
        mode, space = chip_x[t[0]]
        return mode + row_of[t[1]][t[2]], space

    def in_half(t):
        return half_of[0] + row_of[t[0]][t[1]], s

    def in_group(t):
        return half_of[t[0]] + row_of[t[1]][t[2]], s

    def group_source(t):
        return half_of[t[0]] + row_of[(4 - t[1]) % 4][t[2]]

    @pl.when(get_low)
    def _():
        for t in range(16):
            greet((t, below))

    @pl.when(get_high)
    def _():
        for t in range(16):
            greet((t, above))

    for t in PLANE:
        greet(in_plane(t))
    greet(along_z(1))
    greet(along_z(15))

    for i in range(2):
        for z in range(2):
            res[i, z, 0:8, :] = jnp.zeros((8, 128), F32)
            res[i, z, 24:32, :] = jnp.zeros((8, 128), F32)
    loads[0].wait()
    for j in range(8):
        for i in range(2):
            for z in range(2):
                pieces[j, i, 4 * z : 4 * z + 4, :] = res[i, z, 2 * j + 7 : 2 * j + 11, :]
    for i in range(2):
        for z in range(2):
            edges[0, 2 * i + z : 2 * i + z + 1, :] = res[i, z, 23:24, :]
            edges[1, 2 * i + z : 2 * i + z + 1, :] = res[i, z, 8:9, :]
    for load in loads[1:4]:
        load.wait()
    ints[0, :, 0:TERMS] = (part_v[...] % 2) * 16 + part_v[...] // 2
    ints[1, :, 0:TERMS] = term_v[...]
    floats[:, 0:TERMS] = coef_v[...]

    pl.semaphore_wait(barrier, 33 + 2 * low.astype(jnp.int32) + 2 * high.astype(jnp.int32))

    def tell(i):
        for d in (1 << i, 16 - (1 << i)):
            pl.semaphore_signal(ring_sem.at[i], inc=1, device_id=along_z(d), device_id_type=MESH)

    def hear(i):
        pl.semaphore_wait(ring_sem.at[i], 2)

    def main_copy(i):
        to = in_group(GROUP[i])
        return pltpu.make_async_remote_copy(
            src_ref=pieces.at[row_of[GROUP[i][1]][GROUP[i][2]]], dst_ref=got.at[m], send_sem=main_ss, recv_sem=main_rs.at[i],
            device_id=to, device_id_type=MESH,
        )

    def edge_copy(up, half):
        to = (half * 8, above) if up else (half * 8 + 7, below)
        return pltpu.make_async_remote_copy(
            src_ref=edges.at[0 if up else 1], dst_ref=got_edges.at[m], send_sem=edge_ss.at[(0 if up else 2) + half],
            recv_sem=edge_rs, device_id=to, device_id_type=MESH,
        )

    def kl_copy():
        return pltpu.make_async_remote_copy(
            src_ref=kl_edge, dst_ref=got_kl, send_sem=kle_ss, recv_sem=kle_rs,
            device_id=(m, jnp.where(first, above, below)), device_id_type=MESH,
        )

    def int_copy(i):
        return pltpu.make_async_remote_copy(
            src_ref=ints, dst_ref=got_ints.at[q], send_sem=int_ss, recv_sem=int_rs,
            device_id=in_half(HALF[i]), device_id_type=MESH,
        )

    def float_copy(i):
        return pltpu.make_async_remote_copy(
            src_ref=floats, dst_ref=got_floats.at[q], send_sem=flo_ss, recv_sem=flo_rs,
            device_id=in_half(HALF[i]), device_id_type=MESH,
        )

    def all_of(ref, n, send_sem, recv_sem):
        return pltpu.make_async_remote_copy(
            src_ref=ref.at[pl.ds(0, n)], dst_ref=ref.at[pl.ds(0, n)], send_sem=send_sem, recv_sem=recv_sem,
            device_id=(m, s), device_id_type=MESH,
        )

    @pl.when(high)
    def _():
        edge_copy(True, 0).start()
        edge_copy(True, 1).start()

    @pl.when(low)
    def _():
        edge_copy(False, 0).start()
        edge_copy(False, 1).start()

    for i in range(15):
        main_copy(i).start()
    for i in range(7):
        int_copy(i).start()
        float_copy(i).start()
    tell(0)

    loads[4].wait()
    end = jnp.where(first, 23, 8)
    for z in range(2):
        kl_edge[:, z : z + 1, :] = klv[:, z, pl.ds(end, 1), :]

    @pl.when(put_kl)
    def _():
        kl_copy().start()

    hear(0)
    tell(1)

    for z in range(2):
        for r in range(4):
            cof[:, 4 * z + r : 4 * z + r + 1, :] = klv[:, z, pl.ds(2 * q + 7 + r, 1), :]

    @pl.when(first)
    def _():
        cof[:, 0:1, :] = jnp.zeros((KL, 1, 128), F32)
        cof[:, 4:5, :] = jnp.zeros((KL, 1, 128), F32)

    @pl.when(last)
    def _():
        cof[:, 3:4, :] = jnp.zeros((KL, 1, 128), F32)
        cof[:, 7:8, :] = jnp.zeros((KL, 1, 128), F32)

    lane = lax.broadcasted_iota(jnp.int32, (8, 128), 1)
    sub = lax.broadcasted_iota(jnp.int32, (8, 128), 0)
    inner = jnp.where(lane < 127, 0.5, 0.0).astype(F32)
    border = (0.5 + jnp.where(lane == 0, 0.5, 0.0) + jnp.where(lane == 127, 0.5, 0.0)).astype(F32)
    valid = (sub % 4 == 1) | (sub % 4 == 2)

    def differences(d, tiles):
        for i in range(2):
            v = tiles[i]
            at = 16 * i + d
            ff[at, 0] = v - pltpu.roll(v, 7, 0)
            ff[at, 1] = v - pltpu.roll(v, 127, 1)
            ff[at, 2] = v - pltpu.roll(v, 4, 0)
            ff[at, 3] = v

    differences(m, [pieces[q, 0], pieces[q, 1]])
    got_ints[q] = ints[...]
    got_floats[q] = floats[...]

    @pl.when(get_edge)
    def _():
        kl_copy().wait_recv()

    @pl.when(get_low)
    def _():
        cof[:, 0:1, :] = got_kl[:, 0:1, :]
        cof[:, 4:5, :] = got_kl[:, 1:2, :]

    @pl.when(get_high)
    def _():
        cof[:, 3:4, :] = got_kl[:, 0:1, :]
        cof[:, 7:8, :] = got_kl[:, 1:2, :]

    for k in range(KL):
        a = cof[k]
        aa[k, 0] = 0.5 * (a + pltpu.roll(a, 7, 0))
        aa[k, 1] = inner * (a + pltpu.roll(a, 127, 1))
        aa[k, 2] = 0.5 * (a + pltpu.roll(a, 4, 0))
        aa[k, 3] = border * a

    hear(1)
    tell(2)
    all_of(got_ints, 7, int_ss, int_rs).wait_recv()
    all_of(got_floats, 7, flo_ss, flo_rs).wait_recv()
    to_smem = [
        pltpu.make_async_copy(got_ints, int_s, smem_sem.at[0]),
        pltpu.make_async_copy(got_floats, float_s, smem_sem.at[1]),
    ]
    for copy in to_smem:
        copy.start()

    def take(i):
        main_copy(i).wait_recv()
        d = group_source(GROUP[i])
        differences(d, [got[d, 0], got[d, 1]])

    for i in range(14, 7, -1):
        take(i)
    for copy in to_smem:
        copy.wait()

    def weigh(h, carry):
        for i in range(2):
            for e in range(TERMS):
                k = int_s[h, 1, i, e]
                w = float_s[h, i, e]
                for d in range(4):
                    wa[2 * h + i, e, d] = w * aa[k, d]
        return carry

    lax.fori_loop(0, 8, weigh, 0)
    for i in range(7, -1, -1):
        take(i)

    @pl.when(get_edge)
    def _():
        all_of(got_edges, 16, edge_ss.at[0], edge_rs).wait_recv()

    @pl.when(get_low)
    def _():
        for i in range(2):
            for z in range(2):
                at = (pl.ds(16 * i, 16), 0, slice(4 * z, 4 * z + 1))
                ff[at] = ff[at] + got_edges[:, 2 * i + z : 2 * i + z + 1, :]

    @pl.when(get_high)
    def _():
        for i in range(2):
            for z in range(2):
                at = (pl.ds(16 * i, 16), 0, slice(4 * z + 2, 4 * z + 3))
                ff[at] = ff[at] - got_edges[:, 2 * i + z : 2 * i + z + 1, :]

    def four_modes(h, carry):
        norm, curve, energy = carry
        for j in range(4):
            n = 4 * h + j
            own = 16 * (j % 2) + g * 8 + 2 * h + j // 2
            flux_x = aa[0, 0] * ff[own, 0]
            flux_y = aa[0, 1] * ff[own, 1]
            rest = aa[0, 2] * ff[own, 2] + aa[0, 3] * ff[own, 3]
            for e in range(TERMS):
                p = int_s[2 * h + j // 2, 0, j % 2, e]
                flux_x += wa[n, e, 0] * ff[p, 0]
                flux_y += wa[n, e, 1] * ff[p, 1]
                rest += wa[n, e, 2] * ff[p, 2] + wa[n, e, 3] * ff[p, 3]
            out = rest + (flux_x - pltpu.roll(flux_x, 1, 0)) + (flux_y - pltpu.roll(flux_y, 1, 1))
            img[n] = out
            out = jnp.where(valid, out, 0.0)
            v = jnp.where(valid, ff[own, 3], 0.0)
            norm, curve, energy = norm + v * v, curve + v * out, energy + out * out
        return norm, curve, energy

    zero = jnp.zeros((8, 128), F32)
    parts = lax.fori_loop(0, 4, four_modes, (zero, zero, zero))

    sum_a[...] = jnp.zeros((4, 128), F32)
    for i in range(3):
        sum_a[i : i + 1, :] = jnp.sum(parts[i], axis=0, keepdims=True)

    def a_copy(t):
        return pltpu.make_async_remote_copy(
            src_ref=sum_a, dst_ref=sums_a.at[own_plane], send_sem=a_ss, recv_sem=a_rs,
            device_id=in_plane(t), device_id_type=MESH,
        )

    def b_copy(d):
        return pltpu.make_async_remote_copy(
            src_ref=sum_b, dst_ref=sums_b.at[z_at], send_sem=b_ss, recv_sem=b_rs,
            device_id=along_z(d), device_id_type=MESH,
        )

    def back_copy(t):
        return pltpu.make_async_remote_copy(
            src_ref=img.at[pl.ds(2 * row_of[t[0]][t[1]], 2)], dst_ref=back.at[q], send_sem=back_ss, recv_sem=back_rs,
            device_id=in_half(t), device_id_type=MESH,
        )

    for t in PLANE:
        a_copy(t).start()
    sums_a[own_plane] = sum_a[...]
    hear(2)
    all_of(sums_a, 31, a_ss, a_rs).wait_recv()
    sum_b[...] = jnp.sum(sums_a[...], axis=0)
    for d in RING:
        b_copy(d).start()
    for t in HALF:
        back_copy(t).start()
    sums_b[z_at] = sum_b[...]
    back[q] = img[pl.ds(2 * q, 2)]

    all_of(back, 7, back_ss, back_rs).wait_recv()
    for i in range(2):
        for z in range(2):
            for h in range(2):
                tile = pltpu.roll(back[4 * h, i], 7 - 4 * z, 0)
                for j in range(1, 4):
                    tile = jnp.where(sub // 2 == j, pltpu.roll(back[4 * h + j, i], (2 * j + 7 - 4 * z) % 8, 0), tile)
                image_ref[i, z, 8 * h : 8 * h + 8, :] = tile
    loads[5].wait()

    all_of(got, 15, main_ss, main_rs.at[0]).wait_send()
    all_of(got_ints, 7, int_ss, int_rs).wait_send()
    all_of(got_floats, 7, flo_ss, flo_rs).wait_send()
    all_of(back, 7, back_ss, back_rs).wait_send()
    all_of(sums_a, 31, a_ss, a_rs).wait_send()

    @pl.when(put_kl)
    def _():
        kl_copy().wait_send()

    @pl.when(high)
    def _():
        edge_copy(True, 0).wait_send()
        edge_copy(True, 1).wait_send()

    @pl.when(low)
    def _():
        edge_copy(False, 0).wait_send()
        edge_copy(False, 1).wait_send()

    all_of(sums_b, 15, b_ss, b_rs).wait_recv()
    sums = jnp.sum(jnp.sum(sums_b[...], axis=0), axis=1, keepdims=True)
    norm, curve, energy = sums[0:1], sums[1:2], sums[2:3]
    step = curve / (energy + EPS)
    norm_new = jnp.maximum(norm - 2.0 * step * curve + step * step * energy, 0.0)
    beta = norm_new / (norm + EPS)
    for i in range(2):
        for z in range(2):
            for h in range(2):
                rows = pl.ds(8 * h, 8)
                r = res[i, z, 8 + 8 * h : 16 + 8 * h, :]
                sol_ref[i, z, rows, :] = sol[i, z, rows, :] + step * r
                r_new = r - step * image_ref[i, z, rows, :]
                res_ref[i, z, rows, :] = r_new
                dir_ref[i, z, rows, :] = r_new + beta * r
    all_of(sums_b, 15, b_ss, b_rs).wait_send()


def deliver(*refs):
    sem = refs[8]
    copies = [pltpu.make_async_copy(refs[i], refs[4 + i], sem.at[i]) for i in range(4)]
    for copy in copies:
        copy.start()
    for copy in copies:
        copy.wait()


def on_device(residual, solution, kl_terms, partner, kl_index, coefficient):
    vmem = pl.BlockSpec(memory_space=pltpu.VMEM)
    anywhere = pl.BlockSpec(memory_space=pl.ANY)
    dma = pltpu.SemaphoreType.DMA
    field = pltpu.VMEM(residual.shape, F32)
    i32 = jnp.int32
    results = pl.pallas_call(
        galerkin,
        out_shape=(field,) * 4,
        in_specs=[anywhere] * 6,
        out_specs=(vmem,) * 4,
        scratch_shapes=[
            pltpu.VMEM((2, 2, 32, 128), F32),
            pltpu.VMEM((2, 2, 16, 128), F32),
            pltpu.VMEM((KL, 2, 32, 128), F32),
            pltpu.VMEM((2, TERMS), i32),
            pltpu.VMEM((2, TERMS), i32),
            pltpu.VMEM((2, TERMS), F32),
            pltpu.VMEM((8, 2, 8, 128), F32),
            pltpu.VMEM((2, 4, 128), F32),
            pltpu.VMEM((KL, 2, 128), F32),
            pltpu.VMEM((2, 2, 128), i32),
            pltpu.VMEM((2, 128), F32),
            pltpu.VMEM((16, 2, 8, 128), F32),
            pltpu.VMEM((16, 4, 128), F32),
            pltpu.VMEM((KL, 2, 128), F32),
            pltpu.VMEM((8, 2, 2, 128), i32),
            pltpu.VMEM((8, 2, 128), F32),
            pltpu.SMEM((8, 2, 2, 128), i32),
            pltpu.SMEM((8, 2, 128), F32),
            pltpu.VMEM((KL, 8, 128), F32),
            pltpu.VMEM((KL, 4, 8, 128), F32),
            pltpu.VMEM((16, TERMS, 4, 8, 128), F32),
            pltpu.VMEM((MODES, 4, 8, 128), F32),
            pltpu.VMEM((16, 8, 128), F32),
            pltpu.VMEM((8, 2, 8, 128), F32),
            pltpu.VMEM((4, 128), F32),
            pltpu.VMEM((32, 4, 128), F32),
            pltpu.VMEM((4, 128), F32),
            pltpu.VMEM((16, 4, 128), F32),
            dma((6,)),
            dma, dma((15,)),
            dma((4,)), dma,
            dma, dma,
            dma, dma,
            dma, dma,
            dma((2,)),
            dma, dma,
            dma, dma,
            dma, dma,
            pltpu.SemaphoreType.REGULAR((3,)),
        ],
        compiler_params=pltpu.CompilerParams(
            collective_id=0, has_side_effects=True, vmem_limit_bytes=60 << 20
        ),
        name="galerkin",
    )(residual, solution, kl_terms, partner, kl_index, coefficient)
    return pl.pallas_call(
        deliver,
        out_shape=(jax.ShapeDtypeStruct(residual.shape, F32),) * 4,
        in_specs=[vmem] * 4,
        out_specs=(anywhere,) * 4,
        scratch_shapes=[dma((4,))],
        compiler_params=pltpu.CompilerParams(vmem_limit_bytes=60 << 20),
        name="deliver",
    )(*(pltpu.with_memory_space_constraint(a, pltpu.VMEM) for a in results))


def solution(mesh):
    field = P("mode", None, "space", None)
    row = P("mode", None)
    return jax.shard_map(
        on_device,
        mesh=mesh,
        in_specs=(field, field, P(None, None, "space", None), row, row, row),
        out_specs=(field, field, field, field),
        check_vma=False,
    )
```

time: 40 us -> 35 us (0.88)
  Pallas kernels: 39.3 us -> 34.2 us
    pallas_call x1, Pallas kernels: 38.6 us -> 33.5 us  [on_device(): pl.pallas_call(galerkin, out_shape=(field,) * 4, in_specs=[anywhere] * 6,...]
where the time goes in v3:
time: 35 us; the launch traced here: 34.8 us
  Pallas kernels  34.2 us (98%)
  between operations  0.64 us (2%)
    pallas_call x1, Pallas kernels, on_device(): pl.pallas_call(galerkin, out_shape=(field,) * 4, in_specs=[anywhere] * 6,...  33.5 us

profile of v3, /device:TPU:1, one launch (start us, length us, event | category | flops | bytes accessed | tf_op | source)
XLA Modules:
  0.0 34.8 jit_solution(5736030033699804227)
XLA Ops:
  0.6 33.5 %galerkin.1 = (f32[2,2,16,128]{3,2,1,0:T(8,128)S(1)}, f32[2,2,16,128]{3,2,1,0:T(8,128)S(1)}, f32[2,2,16,128]{3,2,1,0:T(8,128)S(1)}, f32[2,2,16,128]{3,2,1,0:T(8,128)S(1)}) custom-call(f32[2,2,16,128]{3,2,1,0:T(8,128)} %res_hbm.1, f32[2,2,16,128]{3,2,1,0:T(8,128)} %sol_hbm.1, f32[21,2,16,128]{3,2,1,0:T(8,128)} %kl_hbm.1, s32[2,24]{1,0:T(2,128)} %part_hbm.1, ...), custom_call_target="tpu_custom_call" | custom-call | tf_op jit(solution)/shard_map/galerkin/pallas_call | solution.py:427
  34.1 0.7 %deliver.1 = (f32[2,2,16,128]{3,2,1,0:T(8,128)}, f32[2,2,16,128]{3,2,1,0:T(8,128)}, f32[2,2,16,128]{3,2,1,0:T(8,128)}, f32[2,2,16,128]{3,2,1,0:T(8,128)}) custom-call(f32[2,2,16,128]{3,2,1,0:T(8,128)S(1)} %get-tuple-element.8.refs_0_, f32[2,2,16,128]{3,2,1,0:T(8,128)S(1)} %get-tuple-element.9.refs_1_, f32[2,2,16,128]{3,2,1,0:T(8,128)S(1)} %get-tuple-element.10.refs_2_, ...), custom_call_target="tpu_custom_call" | custom-call | tf_op jit(solution)/shard_map/deliver/pallas_call | solution.py:478

commit v4 on v3

v4 whole, which is shorter than its diff:
```python
import jax
import jax.numpy as jnp
from jax import lax
from jax.experimental import pallas as pl
from jax.experimental.pallas import tpu as pltpu
from jax.sharding import PartitionSpec as P

EPS = 1e-6
MESH = pl.DeviceIdType.MESH
KL, TERMS, MODES = 21, 24, 32
F32 = jnp.float32


def hops(dy):
    return min(dy, 4 - dy)


SHIFTS = sorted(((b, d) for b in range(4) for d in (0, 1)), key=lambda t: (-hops(t[0]), -t[1]))
RING = [8, 7, 9, 6, 10, 5, 11, 4, 12, 3, 13, 2, 14, 1, 15]


def chunk(row):
    return jnp.where(row == 0, 0, jnp.where(row == 1, 7, row - 1))


def galerkin(
    res_hbm, sol_hbm, kl_hbm, part_hbm, term_hbm, coef_hbm,
    image_ref, sol_ref, res_ref, dir_ref,
    res, sol, klv, part_v, term_v, coef_v,
    pieces, edges, kl_edge, ints, floats,
    got, got_edges, got_kl, got_ints, got_floats, int_s, float_s,
    cof, aa, wa, ff, flux, img, back, sum_a, sums_a, sum_b, sums_b,
    in_sem, main_ss, main_rs, edge_ss, edge_rs, kle_ss, kle_rs,
    int_ss, int_rs, flo_ss, flo_rs, smem_sem,
    a_ss, a_rs, b_ss, b_rs, back_ss, back_rs, ring_sem, here_sem,
):
    m, s = lax.axis_index("mode"), lax.axis_index("space")
    g, q = m // 8, chunk(m % 8)
    y, c, xl, z_at = (m // 2) % 4, m % 2, s // 16, s % 16
    ys = [(y + b) % 4 for b in range(4)]
    cs = [c, 1 - c]
    row_of = [[ys[b] * 2 + cs[d] for d in range(2)] for b in range(4)]
    across = (1 - xl) * 16 + z_at
    works, sends = g == 0, g == 1
    low, high = s > 0, s < 31
    first, last = m == 0, m == 1
    get_low, get_high = first & low, last & high
    get_edge = get_low | get_high
    put_kl = (first & high) | (last & low)
    below, above = jnp.maximum(s - 1, 0), jnp.minimum(s + 1, 31)

    loads = [
        pltpu.make_async_copy(a, b, in_sem.at[i])
        for i, (a, b) in enumerate(
            (
                (res_hbm, res.at[:, :, 8:24, :]),
                (part_hbm, part_v),
                (term_hbm, term_v),
                (coef_hbm, coef_v),
                (kl_hbm, klv.at[:, :, 8:24, :]),
                (sol_hbm, sol),
            )
        )
    ]
    for load in loads[:4]:
        load.start()

    barrier = pltpu.get_barrier_semaphore()

    def greet(device):
        pl.semaphore_signal(barrier, inc=1, device_id=device, device_id_type=MESH)

    def along_z(d):
        return m, xl * 16 + (z_at + d) % 16

    @pl.when(works)
    def _():
        for b, d in SHIFTS:
            greet((8 + row_of[b][d], s))
            greet((8 + row_of[b][d], across))
        for b, d in SHIFTS:
            greet((row_of[b][d], across))
            if b or d:
                greet((row_of[b][d], s))

    @pl.when(get_low)
    def _():
        for t in range(15, -1, -1):
            greet((t, below))

    @pl.when(get_high)
    def _():
        for t in range(15, -1, -1):
            greet((t, above))

    greet(along_z(1))
    greet(along_z(15))
    for load in loads[4:]:
        load.start()

    for i in range(2):
        for z in range(2):
            res[i, z, 0:8, :] = jnp.zeros((8, 128), F32)
            res[i, z, 24:32, :] = jnp.zeros((8, 128), F32)
    for load in loads[:4]:
        load.wait()
    ints[0, :, 0:TERMS] = (part_v[...] % 2) * 16 + part_v[...] // 2
    ints[1, :, 0:TERMS] = term_v[...]
    floats[:, 0:TERMS] = coef_v[...]
    for j in range(8):
        for i in range(2):
            for z in range(2):
                pieces[j, i, 4 * z : 4 * z + 4, :] = res[i, z, 2 * j + 7 : 2 * j + 11, :]
    for i in range(2):
        for z in range(2):
            edges[0, 2 * i + z : 2 * i + z + 1, :] = res[i, z, 23:24, :]
            edges[1, 2 * i + z : 2 * i + z + 1, :] = res[i, z, 8:9, :]

    pl.semaphore_wait(barrier, 17 + g + low.astype(jnp.int32) + high.astype(jnp.int32))

    def tell(i):
        for d in (1 << i, 16 - (1 << i)):
            pl.semaphore_signal(ring_sem.at[i], inc=1, device_id=along_z(d), device_id_type=MESH)

    def hear(i):
        pl.semaphore_wait(ring_sem.at[i], 2)

    def copy_to(src, dst, send_sem, recv_sem, device):
        return pltpu.make_async_remote_copy(
            src_ref=src, dst_ref=dst, send_sem=send_sem, recv_sem=recv_sem, device_id=device, device_id_type=MESH
        )

    def main_copy(i):
        to = row_of[SHIFTS[i][0]][SHIFTS[i][1]]
        return copy_to(pieces.at[chunk(to)], got.at[m], main_ss, main_rs.at[g * 8 + i], (to, s))

    def int_copy(i):
        return copy_to(ints, got_ints.at[m], int_ss, int_rs.at[g], (row_of[SHIFTS[i][0]][SHIFTS[i][1]], s))

    def float_copy(i):
        return copy_to(floats, got_floats.at[m], flo_ss, flo_rs.at[g], (row_of[SHIFTS[i][0]][SHIFTS[i][1]], s))

    def edge_copy(up):
        to = (0, above) if up else (1, below)
        return copy_to(edges.at[1 - up], got_edges.at[m], edge_ss.at[up], edge_rs, to)

    def kl_copy():
        return copy_to(kl_edge, got_kl, kle_ss, kle_rs, (m, jnp.where(first, above, below)))

    def all_of(ref, n, send_sem, recv_sem):
        return copy_to(ref.at[pl.ds(0, n)], ref.at[pl.ds(0, n)], send_sem, recv_sem, (m, s))

    @pl.when(high)
    def _():
        edge_copy(1).start()

    @pl.when(low)
    def _():
        edge_copy(0).start()

    for i in range(7):
        int_copy(i).start()
        float_copy(i).start()
    for i in range(7):
        main_copy(i).start()

    @pl.when(sends)
    def _():
        int_copy(7).start()
        float_copy(7).start()
        main_copy(7).start()

    tell(0)

    @pl.when(sends)
    def _():
        for t in range(8):
            for to in ((t, s), (t, across)):
                pl.semaphore_signal(here_sem, inc=1, device_id=to, device_id_type=MESH)
        hear(0)
        tell(1)
        hear(1)
        tell(2)

    lane = lax.broadcasted_iota(jnp.int32, (8, 128), 1)
    sub = lax.broadcasted_iota(jnp.int32, (8, 128), 0)
    row = sub % 4
    inner = jnp.where(lane < 127, 0.5, 0.0).astype(F32)
    border = (0.5 + jnp.where(lane == 0, 0.5, 0.0) + jnp.where(lane == 127, 0.5, 0.0)).astype(F32)
    valid = (row == 1) | (row == 2)

    def faces(x, z):
        return jnp.where(sub == 3, pltpu.roll(z, 2, 0), jnp.where(sub == 7, pltpu.roll(z, 5, 0), x))

    def rows(y, own):
        return jnp.where(row == 0, pltpu.roll(own, 7, 0), jnp.where(row == 3, pltpu.roll(own, 1, 0), y))

    def differences(d, tiles):
        for i in range(2):
            v = tiles[i]
            ff[16 * i + d, 0] = faces(v - pltpu.roll(v, 7, 0), v - pltpu.roll(v, 4, 0))
            ff[16 * i + d, 1] = rows(v - pltpu.roll(v, 127, 1), v)

    def take(a, i):
        copy_to(pieces.at[0], got.at[0], main_ss, main_rs.at[a * 8 + i], (m, s)).wait_recv()
        d = a * 8 + row_of[(4 - SHIFTS[i][0]) % 4][SHIFTS[i][1]]
        differences(d, [got[d, 0], got[d, 1]])

    def weigh(h, carry):
        for i in range(2):
            for e in range(TERMS):
                k = int_s[h, 1, i, e]
                w = float_s[h, i, e]
                wa[2 * h + i, e, 0] = w * aa[k, 0]
                wa[2 * h + i, e, 1] = w * aa[k, 1]
        return carry

    def eight_modes(h, carry):
        for j in range(8):
            n = 8 * h + j
            o, i = 4 * h + j // 2, j % 2
            one = aa[0, 0] * ff[16 * i + o, 0]
            two = aa[0, 1] * ff[16 * i + o, 1]
            for e in range(TERMS):
                p = int_s[o, 0, i, e]
                one += wa[n, e, 0] * ff[p, 0]
                two += wa[n, e, 1] * ff[p, 1]
            flux[n, 0] = one
            flux[n, 1] = two
        return carry

    row_0 = jnp.where(row == 0, 1.0, 0.0).astype(F32)
    row_2 = jnp.where(row == 2, 1.0, 0.0).astype(F32)
    last_sub = jnp.where(sub == 7, 1.0, 0.0).astype(F32)

    def sixteen_modes(h, carry):
        norm, curve, energy = carry
        for j in range(16):
            n = 16 * h + j
            one, two = flux[n, 0], flux[n, 1]
            out = one + two - pltpu.roll(two, 1, 1)
            out += pltpu.roll(row_0 * two - one, 1, 0)
            out += row_2 * pltpu.roll(two - last_sub * one, 7, 0)
            out += jnp.where(sub == 1, pltpu.roll(one, 6, 0), jnp.where(sub == 2, pltpu.roll(one, 3, 0), 0.0))
            out -= jnp.where(sub == 5, pltpu.roll(one, 2, 0), 0.0)
            img[n] = out
            out = jnp.where(valid, out, 0.0)
            v = jnp.where(valid, got[8 * h + j // 2, j % 2], 0.0)
            norm, curve, energy = norm + v * v, curve + v * out, energy + out * out
        return norm, curve, energy

    own_sum = xl * 8 + m % 8

    def a_copy(mode, space):
        return copy_to(sum_a, sums_a.at[own_sum], a_ss, a_rs, (mode, space))

    def to_scalars(a):
        half = pl.ds(8 * a, 8)
        copies = [
            pltpu.make_async_copy(got_ints.at[half], int_s.at[half], smem_sem.at[2 * a]),
            pltpu.make_async_copy(got_floats.at[half], float_s.at[half], smem_sem.at[2 * a + 1]),
        ]
        for copy in copies:
            copy.start()
        return copies

    @pl.when(works)
    def _():
        loads[4].wait()
        end = jnp.where(first, 23, 8)
        for z in range(2):
            kl_edge[:, z : z + 1, :] = klv[:, z, pl.ds(end, 1), :]

        @pl.when(put_kl)
        def _():
            kl_copy().start()

        got_ints[m] = ints[...]
        got_floats[m] = floats[...]
        hear(0)
        tell(1)

        for z in range(2):
            for r in range(4):
                cof[:, 4 * z + r : 4 * z + r + 1, :] = klv[:, z, pl.ds(2 * q + 7 + r, 1), :]

        @pl.when(first)
        def _():
            cof[:, 0:1, :] = jnp.zeros((KL, 1, 128), F32)
            cof[:, 4:5, :] = jnp.zeros((KL, 1, 128), F32)

        @pl.when(last)
        def _():
            cof[:, 3:4, :] = jnp.zeros((KL, 1, 128), F32)
            cof[:, 7:8, :] = jnp.zeros((KL, 1, 128), F32)

        got[m] = pieces[q]
        differences(m, [pieces[q, 0], pieces[q, 1]])

        @pl.when(get_edge)
        def _():
            kl_copy().wait_recv()

        @pl.when(get_low)
        def _():
            cof[:, 0:1, :] = got_kl[:, 0:1, :]
            cof[:, 4:5, :] = got_kl[:, 1:2, :]

        @pl.when(get_high)
        def _():
            cof[:, 3:4, :] = got_kl[:, 0:1, :]
            cof[:, 7:8, :] = got_kl[:, 1:2, :]

        for k in range(KL):
            a = cof[k]
            aa[k, 0] = faces(0.5 * (a + pltpu.roll(a, 7, 0)), 0.5 * (a + pltpu.roll(a, 4, 0)))
            aa[k, 1] = rows(inner * (a + pltpu.roll(a, 127, 1)), border * a)

        hear(1)
        tell(2)
        all_of(got_ints, 7, int_ss, int_rs.at[0]).wait_recv()
        all_of(got_floats, 7, flo_ss, flo_rs.at[0]).wait_recv()
        near = to_scalars(0)
        for i in range(6, -1, -1):
            take(0, i)
        for copy in near:
            copy.wait()
        lax.fori_loop(0, 8, weigh, 0)
        all_of(got_ints, 8, int_ss, int_rs.at[1]).wait_recv()
        all_of(got_floats, 8, flo_ss, flo_rs.at[1]).wait_recv()
        far = to_scalars(1)
        for i in range(7, -1, -1):
            take(1, i)

        @pl.when(get_edge)
        def _():
            all_of(got_edges, 16, edge_ss.at[0], edge_rs).wait_recv()

        @pl.when(get_low)
        def _():
            for i in range(2):
                for z in range(2):
                    at = (pl.ds(16 * i, 16), 0, slice(4 * z, 4 * z + 1))
                    ff[at] = ff[at] + got_edges[:, 2 * i + z : 2 * i + z + 1, :]

        @pl.when(get_high)
        def _():
            for i in range(2):
                for z in range(2):
                    at = (pl.ds(16 * i, 16), 0, slice(4 * z + 2, 4 * z + 3))
                    ff[at] = ff[at] - got_edges[:, 2 * i + z : 2 * i + z + 1, :]

        zero = jnp.zeros((8, 128), F32)
        lax.fori_loop(0, 2, eight_modes, 0)
        for copy in far:
            copy.wait()
        lax.fori_loop(8, 16, weigh, 0)
        lax.fori_loop(2, 4, eight_modes, 0)
        parts = lax.fori_loop(0, 2, sixteen_modes, (zero, zero, zero))

        sum_a[...] = jnp.zeros((4, 128), F32)
        for i in range(3):
            sum_a[i : i + 1, :] = jnp.sum(parts[i], axis=0, keepdims=True)
        pl.semaphore_wait(here_sem, 16)
        for half in (0, 8):
            for b, d in SHIFTS:
                a_copy(half + row_of[b][d], across).start()
                if half or b or d:
                    a_copy(half + row_of[b][d], s).start()
        sums_a[own_sum] = sum_a[...]
        all_of(sums_a, 15, a_ss, a_rs).wait_recv()

    @pl.when(sends)
    def _():
        all_of(sums_a, 16, a_ss, a_rs).wait_recv()

    def b_copy(d):
        return copy_to(sum_b, sums_b.at[z_at], b_ss, b_rs, along_z(d))

    def back_copy(to):
        return copy_to(img.at[pl.ds(2 * to, 2)], back.at[q], back_ss, back_rs, (to, s))

    sum_b[...] = jnp.sum(sums_a[...], axis=0)
    hear(2)
    for d in RING:
        b_copy(d).start()
    sums_b[z_at] = sum_b[...]

    @pl.when(works)
    def _():
        for b, d in SHIFTS:
            back_copy(8 + row_of[b][d]).start()
            if b or d:
                back_copy(row_of[b][d]).start()
        back[q] = img[pl.ds(2 * m, 2)]
        all_of(back, 7, back_ss, back_rs).wait_recv()

    @pl.when(sends)
    def _():
        all_of(back, 8, back_ss, back_rs).wait_recv()

    for i in range(2):
        for z in range(2):
            for h in range(2):
                tile = pltpu.roll(back[4 * h, i], 7 - 4 * z, 0)
                for j in range(1, 4):
                    tile = jnp.where(sub // 2 == j, pltpu.roll(back[4 * h + j, i], (2 * j + 7 - 4 * z) % 8, 0), tile)
                image_ref[i, z, 8 * h : 8 * h + 8, :] = tile
    loads[5].wait()

    @pl.when(works)
    def _():
        all_of(pieces, 7, main_ss, main_rs.at[0]).wait_send()
        all_of(got_ints, 7, int_ss, int_rs.at[0]).wait_send()
        all_of(got_floats, 7, flo_ss, flo_rs.at[0]).wait_send()
        all_of(got, 15, back_ss, back_rs).wait_send()
        all_of(sums_b, 16, a_ss, a_rs).wait_send()
        all_of(sums_b, 15, a_ss, a_rs).wait_send()

    @pl.when(sends)
    def _():
        loads[4].wait()
        all_of(pieces, 8, main_ss, main_rs.at[0]).wait_send()
        all_of(got_ints, 8, int_ss, int_rs.at[0]).wait_send()
        all_of(got_floats, 8, flo_ss, flo_rs.at[0]).wait_send()

    @pl.when(put_kl)
    def _():
        kl_copy().wait_send()

    @pl.when(high)
    def _():
        edge_copy(1).wait_send()

    @pl.when(low)
    def _():
        edge_copy(0).wait_send()

    all_of(sums_b, 15, b_ss, b_rs).wait_recv()
    sums = jnp.sum(jnp.sum(sums_b[...], axis=0), axis=1, keepdims=True)
    norm, curve, energy = sums[0:1], sums[1:2], sums[2:3]
    step = curve / (energy + EPS)
    norm_new = jnp.maximum(norm - 2.0 * step * curve + step * step * energy, 0.0)
    beta = norm_new / (norm + EPS)
    for i in range(2):
        for z in range(2):
            for h in range(2):
                at = pl.ds(8 * h, 8)
                r = res[i, z, 8 + 8 * h : 16 + 8 * h, :]
                sol_ref[i, z, at, :] = sol[i, z, at, :] + step * r
                r_new = r - step * image_ref[i, z, at, :]
                res_ref[i, z, at, :] = r_new
                dir_ref[i, z, at, :] = r_new + beta * r
    all_of(sums_b, 15, b_ss, b_rs).wait_send()


def deliver(*refs):
    sem = refs[8]
    copies = [pltpu.make_async_copy(refs[i], refs[4 + i], sem.at[i]) for i in range(4)]
    for copy in copies:
        copy.start()
    for copy in copies:
        copy.wait()


def on_device(residual, solution, kl_terms, partner, kl_index, coefficient):
    vmem = pl.BlockSpec(memory_space=pltpu.VMEM)
    anywhere = pl.BlockSpec(memory_space=pl.ANY)
    dma = pltpu.SemaphoreType.DMA
    field = pltpu.VMEM(residual.shape, F32)
    i32 = jnp.int32
    results = pl.pallas_call(
        galerkin,
        out_shape=(field,) * 4,
        in_specs=[anywhere] * 6,
        out_specs=(vmem,) * 4,
        scratch_shapes=[
            pltpu.VMEM((2, 2, 32, 128), F32),
            pltpu.VMEM((2, 2, 16, 128), F32),
            pltpu.VMEM((KL, 2, 32, 128), F32),
            pltpu.VMEM((2, TERMS), i32),
            pltpu.VMEM((2, TERMS), i32),
            pltpu.VMEM((2, TERMS), F32),
            pltpu.VMEM((8, 2, 8, 128), F32),
            pltpu.VMEM((2, 4, 128), F32),
            pltpu.VMEM((KL, 2, 128), F32),
            pltpu.VMEM((2, 2, 128), i32),
            pltpu.VMEM((2, 128), F32),
            pltpu.VMEM((16, 2, 8, 128), F32),
            pltpu.VMEM((16, 4, 128), F32),
            pltpu.VMEM((KL, 2, 128), F32),
            pltpu.VMEM((16, 2, 2, 128), i32),
            pltpu.VMEM((16, 2, 128), F32),
            pltpu.SMEM((16, 2, 2, 128), i32),
            pltpu.SMEM((16, 2, 128), F32),
            pltpu.VMEM((KL, 8, 128), F32),
            pltpu.VMEM((KL, 2, 8, 128), F32),
            pltpu.VMEM((MODES, TERMS, 2, 8, 128), F32),
            pltpu.VMEM((MODES, 2, 8, 128), F32),
            pltpu.VMEM((MODES, 2, 8, 128), F32),
            pltpu.VMEM((MODES, 8, 128), F32),
            pltpu.VMEM((8, 2, 8, 128), F32),
            pltpu.VMEM((4, 128), F32),
            pltpu.VMEM((16, 4, 128), F32),
            pltpu.VMEM((4, 128), F32),
            pltpu.VMEM((16, 4, 128), F32),
            dma((6,)),
            dma, dma((16,)),
            dma((2,)), dma,
            dma, dma,
            dma, dma((2,)),
            dma, dma((2,)),
            dma((4,)),
            dma, dma,
            dma, dma,
            dma, dma,
            pltpu.SemaphoreType.REGULAR((3,)),
            pltpu.SemaphoreType.REGULAR,
        ],
        compiler_params=pltpu.CompilerParams(
            collective_id=0, has_side_effects=True, vmem_limit_bytes=60 << 20
        ),
        name="galerkin",
    )(residual, solution, kl_terms, partner, kl_index, coefficient)
    return pl.pallas_call(
        deliver,
        out_shape=(jax.ShapeDtypeStruct(residual.shape, F32),) * 4,
        in_specs=[vmem] * 4,
        out_specs=(anywhere,) * 4,
        scratch_shapes=[dma((4,))],
        compiler_params=pltpu.CompilerParams(vmem_limit_bytes=60 << 20),
        name="deliver",
    )(*(pltpu.with_memory_space_constraint(a, pltpu.VMEM) for a in results))


def solution(mesh):
    field = P("mode", None, "space", None)
    row = P("mode", None)
    return jax.shard_map(
        on_device,
        mesh=mesh,
        in_specs=(field, field, P(None, None, "space", None), row, row, row),
        out_specs=(field, field, field, field),
        check_vma=False,
    )
```

time: 35 us -> 34.7 us (level)
  Pallas kernels: 34.2 us -> 33.7 us
    pallas_call x1, Pallas kernels: 33.5 us -> 33 us  [on_device(): pl.pallas_call(galerkin, out_shape=(field,) * 4, in_specs=[anywhere] * 6,...]
where the time goes in v4:
time: 34.7 us; the launch traced here: 34.3 us
  Pallas kernels  33.7 us (97%)
  between operations  0.64 us (2%)
    pallas_call x1, Pallas kernels, on_device(): pl.pallas_call(galerkin, out_shape=(field,) * 4, in_specs=[anywhere] * 6,...  33 us

profile of v4, /device:TPU:1, one launch (start us, length us, event | category | flops | bytes accessed | tf_op | source)
XLA Modules:
  0.0 34.3 jit_solution(878640120601276659)
XLA Ops:
  0.6 33.0 %galerkin.1 = (f32[2,2,16,128]{3,2,1,0:T(8,128)S(1)}, f32[2,2,16,128]{3,2,1,0:T(8,128)S(1)}, f32[2,2,16,128]{3,2,1,0:T(8,128)S(1)}, f32[2,2,16,128]{3,2,1,0:T(8,128)S(1)}) custom-call(f32[2,2,16,128]{3,2,1,0:T(8,128)} %res_hbm.1, f32[2,2,16,128]{3,2,1,0:T(8,128)} %sol_hbm.1, f32[21,2,16,128]{3,2,1,0:T(8,128)} %kl_hbm.1, s32[2,24]{1,0:T(2,128)} %part_hbm.1, ...), custom_call_target="tpu_custom_call" | custom-call | tf_op jit(solution)/shard_map/galerkin/pallas_call | solution.py:472
  33.6 0.7 %deliver.1 = (f32[2,2,16,128]{3,2,1,0:T(8,128)}, f32[2,2,16,128]{3,2,1,0:T(8,128)}, f32[2,2,16,128]{3,2,1,0:T(8,128)}, f32[2,2,16,128]{3,2,1,0:T(8,128)}) custom-call(f32[2,2,16,128]{3,2,1,0:T(8,128)S(1)} %get-tuple-element.8.refs_0_, f32[2,2,16,128]{3,2,1,0:T(8,128)S(1)} %get-tuple-element.9.refs_1_, f32[2,2,16,128]{3,2,1,0:T(8,128)S(1)} %get-tuple-element.10.refs_2_, ...), custom_call_target="tpu_custom_call" | custom-call | tf_op jit(solution)/shard_map/deliver/pallas_call | solution.py:525

commit v5 on v4

--- a/solution.py
+++ b/solution.py
@@ -11,16 +11,12 @@
 F32 = jnp.float32
 
 
-def hops(dy):
-    return min(dy, 4 - dy)
-
-
-SHIFTS = sorted(((b, d) for b in range(4) for d in (0, 1)), key=lambda t: (-hops(t[0]), -t[1]))
+FLIPS = [(a, b, d) for a in (1, 0) for b in (1, 0) for d in (1, 0)]
 RING = [8, 7, 9, 6, 10, 5, 11, 4, 12, 3, 13, 2, 14, 1, 15]
 
 
-def chunk(row):
-    return jnp.where(row == 0, 0, jnp.where(row == 1, 7, row - 1))
+def chunk(r):
+    return jnp.where(r == 0, 0, jnp.where(r == 1, 7, r - 1))
 
 
 def galerkin(
@@ -35,11 +31,13 @@
     a_ss, a_rs, b_ss, b_rs, back_ss, back_rs, ring_sem, here_sem,
 ):
     m, s = lax.axis_index("mode"), lax.axis_index("space")
-    g, q = m // 8, chunk(m % 8)
-    y, c, xl, z_at = (m // 2) % 4, m % 2, s // 16, s % 16
-    ys = [(y + b) % 4 for b in range(4)]
-    cs = [c, 1 - c]
-    row_of = [[ys[b] * 2 + cs[d] for d in range(2)] for b in range(4)]
+    xh, y, c, xl, z_at = m // 8, (m // 2) % 4, m % 2, s // 16, s % 16
+    g, yb = y // 2, y % 2
+    r = xh * 4 + yb * 2 + c
+    slot, q = g * 8 + r, chunk(r)
+    r_of = {f: (1 - xh if f[0] else xh) * 4 + (1 - yb if f[1] else yb) * 2 + (1 - c if f[2] else c) for f in FLIPS}
+    mode_of = {f: (1 - xh if f[0] else xh) * 8 + (1 - yb if f[1] else yb) * 2 + (1 - c if f[2] else c) for f in FLIPS}
+    SELF = FLIPS[7]
     across = (1 - xl) * 16 + z_at
     works, sends = g == 0, g == 1
     low, high = s > 0, s < 31
@@ -75,13 +73,13 @@
 
     @pl.when(works)
     def _():
-        for b, d in SHIFTS:
-            greet((8 + row_of[b][d], s))
-            greet((8 + row_of[b][d], across))
-        for b, d in SHIFTS:
-            greet((row_of[b][d], across))
-            if b or d:
-                greet((row_of[b][d], s))
+        for f in FLIPS:
+            greet((mode_of[f] + 4, s))
+            greet((mode_of[f] + 4, across))
+        for f in FLIPS:
+            greet((mode_of[f], across))
+            if f != SELF:
+                greet((mode_of[f], s))
 
     @pl.when(get_low)
     def _():
@@ -104,7 +102,8 @@
             res[i, z, 24:32, :] = jnp.zeros((8, 128), F32)
     for load in loads[:4]:
         load.wait()
-    ints[0, :, 0:TERMS] = (part_v[...] % 2) * 16 + part_v[...] // 2
+    p = part_v[...]
+    ints[0, :, 0:TERMS] = (p % 2) * 16 + (p // 8) % 2 * 8 + p // 16 * 4 + p // 2 % 4
     ints[1, :, 0:TERMS] = term_v[...]
     floats[:, 0:TERMS] = coef_v[...]
     for j in range(8):
@@ -131,18 +130,18 @@
         )
 
     def main_copy(i):
-        to = row_of[SHIFTS[i][0]][SHIFTS[i][1]]
-        return copy_to(pieces.at[chunk(to)], got.at[m], main_ss, main_rs.at[g * 8 + i], (to, s))
+        f = FLIPS[i]
+        return copy_to(pieces.at[chunk(r_of[f])], got.at[slot], main_ss, main_rs.at[g * 8 + i], (mode_of[f], s))
 
     def int_copy(i):
-        return copy_to(ints, got_ints.at[m], int_ss, int_rs.at[g], (row_of[SHIFTS[i][0]][SHIFTS[i][1]], s))
+        return copy_to(ints, got_ints.at[slot], int_ss, int_rs.at[g], (mode_of[FLIPS[i]], s))
 
     def float_copy(i):
-        return copy_to(floats, got_floats.at[m], flo_ss, flo_rs.at[g], (row_of[SHIFTS[i][0]][SHIFTS[i][1]], s))
+        return copy_to(floats, got_floats.at[slot], flo_ss, flo_rs.at[g], (mode_of[FLIPS[i]], s))
 
     def edge_copy(up):
         to = (0, above) if up else (1, below)
-        return copy_to(edges.at[1 - up], got_edges.at[m], edge_ss.at[up], edge_rs, to)
+        return copy_to(edges.at[1 - up], got_edges.at[slot], edge_ss.at[up], edge_rs, to)
 
     def kl_copy():
         return copy_to(kl_edge, got_kl, kle_ss, kle_rs, (m, jnp.where(first, above, below)))
@@ -174,7 +173,7 @@
 
     @pl.when(sends)
     def _():
-        for t in range(8):
+        for t in (0, 1, 2, 3, 8, 9, 10, 11):
             for to in ((t, s), (t, across)):
                 pl.semaphore_signal(here_sem, inc=1, device_id=to, device_id_type=MESH)
         hear(0)
@@ -201,10 +200,12 @@
             ff[16 * i + d, 0] = faces(v - pltpu.roll(v, 7, 0), v - pltpu.roll(v, 4, 0))
             ff[16 * i + d, 1] = rows(v - pltpu.roll(v, 127, 1), v)
 
-    def take(a, i):
-        copy_to(pieces.at[0], got.at[0], main_ss, main_rs.at[a * 8 + i], (m, s)).wait_recv()
-        d = a * 8 + row_of[(4 - SHIFTS[i][0]) % 4][SHIFTS[i][1]]
-        differences(d, [got[d, 0], got[d, 1]])
+    def take(a, places):
+        for i in places:
+            copy_to(pieces.at[0], got.at[0], main_ss, main_rs.at[a * 8 + i], (m, s)).wait_recv()
+        for i in places:
+            d = a * 8 + r_of[FLIPS[i]]
+            differences(d, [got[d, 0], got[d, 1]])
 
     def weigh(h, carry):
         for i in range(2):
@@ -225,6 +226,22 @@
                 p = int_s[o, 0, i, e]
                 one += wa[n, e, 0] * ff[p, 0]
                 two += wa[n, e, 1] * ff[p, 1]
+            flux[n, 0] = one
+            flux[n, 1] = two
+        return carry
+
+    def eight_far_modes(h, carry):
+        for j in range(8):
+            n = 8 * h + j
+            o, i = 4 * h + j // 2, j % 2
+            one = aa[0, 0] * ff[16 * i + o, 0]
+            two = aa[0, 1] * ff[16 * i + o, 1]
+            for e in range(TERMS):
+                p = int_s[o, 0, i, e]
+                k = int_s[o, 1, i, e]
+                w = float_s[o, i, e]
+                one += w * (aa[k, 0] * ff[p, 0])
+                two += w * (aa[k, 1] * ff[p, 1])
             flux[n, 0] = one
             flux[n, 1] = two
         return carry
@@ -249,7 +266,7 @@
             norm, curve, energy = norm + v * v, curve + v * out, energy + out * out
         return norm, curve, energy
 
-    own_sum = xl * 8 + m % 8
+    own_sum = xl * 8 + r
 
     def a_copy(mode, space):
         return copy_to(sum_a, sums_a.at[own_sum], a_ss, a_rs, (mode, space))
@@ -275,8 +292,8 @@
         def _():
             kl_copy().start()
 
-        got_ints[m] = ints[...]
-        got_floats[m] = floats[...]
+        got_ints[slot] = ints[...]
+        got_floats[slot] = floats[...]
         hear(0)
         tell(1)
 
@@ -294,8 +311,8 @@
             cof[:, 3:4, :] = jnp.zeros((KL, 1, 128), F32)
             cof[:, 7:8, :] = jnp.zeros((KL, 1, 128), F32)
 
-        got[m] = pieces[q]
-        differences(m, [pieces[q, 0], pieces[q, 1]])
+        got[slot] = pieces[q]
+        differences(slot, [pieces[q, 0], pieces[q, 1]])
 
         @pl.when(get_edge)
         def _():
@@ -321,16 +338,14 @@
         all_of(got_ints, 7, int_ss, int_rs.at[0]).wait_recv()
         all_of(got_floats, 7, flo_ss, flo_rs.at[0]).wait_recv()
         near = to_scalars(0)
-        for i in range(6, -1, -1):
-            take(0, i)
+        take(0, range(6, -1, -1))
         for copy in near:
             copy.wait()
         lax.fori_loop(0, 8, weigh, 0)
         all_of(got_ints, 8, int_ss, int_rs.at[1]).wait_recv()
         all_of(got_floats, 8, flo_ss, flo_rs.at[1]).wait_recv()
         far = to_scalars(1)
-        for i in range(7, -1, -1):
-            take(1, i)
+        take(1, range(7, -1, -1))
 
         @pl.when(get_edge)
         def _():
@@ -354,19 +369,18 @@
         lax.fori_loop(0, 2, eight_modes, 0)
         for copy in far:
             copy.wait()
-        lax.fori_loop(8, 16, weigh, 0)
-        lax.fori_loop(2, 4, eight_modes, 0)
+        lax.fori_loop(2, 4, eight_far_modes, 0)
         parts = lax.fori_loop(0, 2, sixteen_modes, (zero, zero, zero))
 
         sum_a[...] = jnp.zeros((4, 128), F32)
         for i in range(3):
             sum_a[i : i + 1, :] = jnp.sum(parts[i], axis=0, keepdims=True)
         pl.semaphore_wait(here_sem, 16)
-        for half in (0, 8):
-            for b, d in SHIFTS:
-                a_copy(half + row_of[b][d], across).start()
-                if half or b or d:
-                    a_copy(half + row_of[b][d], s).start()
+        for other in (0, 4):
+            for f in FLIPS:
+                a_copy(mode_of[f] + other, across).start()
+                if other or f != SELF:
+                    a_copy(mode_of[f] + other, s).start()
         sums_a[own_sum] = sum_a[...]
         all_of(sums_a, 15, a_ss, a_rs).wait_recv()
 
@@ -377,8 +391,9 @@
     def b_copy(d):
         return copy_to(sum_b, sums_b.at[z_at], b_ss, b_rs, along_z(d))
 
-    def back_copy(to):
-        return copy_to(img.at[pl.ds(2 * to, 2)], back.at[q], back_ss, back_rs, (to, s))
+    def back_copy(f, other):
+        src = img.at[pl.ds(2 * (r_of[f] + 2 * other), 2)]
+        return copy_to(src, back.at[q], back_ss, back_rs, (mode_of[f] + other, s))
 
     sum_b[...] = jnp.sum(sums_a[...], axis=0)
     hear(2)
@@ -388,11 +403,11 @@
 
     @pl.when(works)
     def _():
-        for b, d in SHIFTS:
-            back_copy(8 + row_of[b][d]).start()
-            if b or d:
-                back_copy(row_of[b][d]).start()
-        back[q] = img[pl.ds(2 * m, 2)]
+        for f in FLIPS:
+            back_copy(f, 4).start()
+            if f != SELF:
+                back_copy(f, 0).start()
+        back[q] = img[pl.ds(2 * slot, 2)]
         all_of(back, 7, back_ss, back_rs).wait_recv()
 
     @pl.when(sends)
@@ -446,11 +461,11 @@
         for z in range(2):
             for h in range(2):
                 at = pl.ds(8 * h, 8)
-                r = res[i, z, 8 + 8 * h : 16 + 8 * h, :]
-                sol_ref[i, z, at, :] = sol[i, z, at, :] + step * r
-                r_new = r - step * image_ref[i, z, at, :]
-                res_ref[i, z, at, :] = r_new
-                dir_ref[i, z, at, :] = r_new + beta * r
+                old = res[i, z, 8 + 8 * h : 16 + 8 * h, :]
+                sol_ref[i, z, at, :] = sol[i, z, at, :] + step * old
+                new = old - step * image_ref[i, z, at, :]
+                res_ref[i, z, at, :] = new
+                dir_ref[i, z, at, :] = new + beta * old
     all_of(sums_b, 15, b_ss, b_rs).wait_send()
 
 
@@ -495,7 +510,7 @@
             pltpu.SMEM((16, 2, 128), F32),
             pltpu.VMEM((KL, 8, 128), F32),
             pltpu.VMEM((KL, 2, 8, 128), F32),
-            pltpu.VMEM((MODES, TERMS, 2, 8, 128), F32),
+            pltpu.VMEM((MODES // 2, TERMS, 2, 8, 128), F32),
             pltpu.VMEM((MODES, 2, 8, 128), F32),
             pltpu.VMEM((MODES, 2, 8, 128), F32),
             pltpu.VMEM((MODES, 8, 128), F32),

time: 34.7 us -> 33.9 us (0.977)
  Pallas kernels: 33.7 us -> 33.1 us
    pallas_call x1, Pallas kernels: 33 us -> 32.4 us  [on_device(): pl.pallas_call(galerkin, out_shape=(field,) * 4, in_specs=[anywhere] * 6,...]
where the time goes in v5:
time: 33.9 us; the launch traced here: 33.7 us
  Pallas kernels  33.1 us (98%)
  between operations  0.64 us (2%)
    pallas_call x1, Pallas kernels, on_device(): pl.pallas_call(galerkin, out_shape=(field,) * 4, in_specs=[anywhere] * 6,...  32.4 us
    pallas_call x1, Pallas kernels, on_device(): pl.pallas_call(deliver, out_shape=(jax.ShapeDtypeStruct(residual.shape, F...  0.69 us

profile of v5, /device:TPU:1, one launch (start us, length us, event | category | flops | bytes accessed | tf_op | source)
XLA Modules:
  0.0 33.7 jit_solution(1593161067442825743)
XLA Ops:
  0.6 32.4 %galerkin.1 = (f32[2,2,16,128]{3,2,1,0:T(8,128)S(1)}, f32[2,2,16,128]{3,2,1,0:T(8,128)S(1)}, f32[2,2,16,128]{3,2,1,0:T(8,128)S(1)}, f32[2,2,16,128]{3,2,1,0:T(8,128)S(1)}) custom-call(f32[2,2,16,128]{3,2,1,0:T(8,128)} %res_hbm.1, f32[2,2,16,128]{3,2,1,0:T(8,128)} %sol_hbm.1, f32[21,2,16,128]{3,2,1,0:T(8,128)} %kl_hbm.1, s32[2,24]{1,0:T(2,128)} %part_hbm.1, ...), custom_call_target="tpu_custom_call" | custom-call | tf_op jit(solution)/shard_map/galerkin/pallas_call | solution.py:487
  33.0 0.7 %deliver.1 = (f32[2,2,16,128]{3,2,1,0:T(8,128)}, f32[2,2,16,128]{3,2,1,0:T(8,128)}, f32[2,2,16,128]{3,2,1,0:T(8,128)}, f32[2,2,16,128]{3,2,1,0:T(8,128)}) custom-call(f32[2,2,16,128]{3,2,1,0:T(8,128)S(1)} %get-tuple-element.8.refs_0_, f32[2,2,16,128]{3,2,1,0:T(8,128)S(1)} %get-tuple-element.9.refs_1_, f32[2,2,16,128]{3,2,1,0:T(8,128)S(1)} %get-tuple-element.10.refs_2_, ...), custom_call_target="tpu_custom_call" | custom-call | tf_op jit(solution)/shard_map/deliver/pallas_call | solution.py:540

commit v6 on v5

--- a/solution.py
+++ b/solution.py
@@ -11,7 +11,7 @@
 F32 = jnp.float32
 
 
-FLIPS = [(a, b, d) for a in (1, 0) for b in (1, 0) for d in (1, 0)]
+FLIPS = [(a, b, d) for a in (1, 0) for b in ((0, 1) if a else (1, 0)) for d in (1, 0)]
 RING = [8, 7, 9, 6, 10, 5, 11, 4, 12, 3, 13, 2, 14, 1, 15]
 
 
@@ -71,6 +71,16 @@
     def along_z(d):
         return m, xl * 16 + (z_at + d) % 16
 
+    @pl.when(get_low)
+    def _():
+        for t in range(15, -1, -1):
+            greet((t, below))
+
+    @pl.when(get_high)
+    def _():
+        for t in range(15, -1, -1):
+            greet((t, above))
+
     @pl.when(works)
     def _():
         for f in FLIPS:
@@ -81,16 +91,6 @@
             if f != SELF:
                 greet((mode_of[f], s))
 
-    @pl.when(get_low)
-    def _():
-        for t in range(15, -1, -1):
-            greet((t, below))
-
-    @pl.when(get_high)
-    def _():
-        for t in range(15, -1, -1):
-            greet((t, above))
-
     greet(along_z(1))
     greet(along_z(15))
     for load in loads[4:]:
@@ -100,6 +100,7 @@
         for z in range(2):
             res[i, z, 0:8, :] = jnp.zeros((8, 128), F32)
             res[i, z, 24:32, :] = jnp.zeros((8, 128), F32)
+            edges[i, z] = jnp.zeros((8, 128), F32)
     for load in loads[:4]:
         load.wait()
     p = part_v[...]
@@ -112,8 +113,8 @@
                 pieces[j, i, 4 * z : 4 * z + 4, :] = res[i, z, 2 * j + 7 : 2 * j + 11, :]
     for i in range(2):
         for z in range(2):
-            edges[0, 2 * i + z : 2 * i + z + 1, :] = res[i, z, 23:24, :]
-            edges[1, 2 * i + z : 2 * i + z + 1, :] = res[i, z, 8:9, :]
+            edges[0, i, 4 * z : 4 * z + 1, :] = res[i, z, 23:24, :]
+            edges[1, i, 4 * z + 2 : 4 * z + 3, :] = -res[i, z, 8:9, :]
 
     pl.semaphore_wait(barrier, 17 + g + low.astype(jnp.int32) + high.astype(jnp.int32))
 
@@ -230,10 +231,27 @@
             flux[n, 1] = two
         return carry
 
-    def eight_far_modes(h, carry):
+    row_0 = jnp.where(row == 0, 1.0, 0.0).astype(F32)
+    row_2 = jnp.where(row == 2, 1.0, 0.0).astype(F32)
+    last_sub = jnp.where(sub == 7, 1.0, 0.0).astype(F32)
+
+    def finish(n, v, sums):
+        norm, curve, energy = sums
+        one, two = flux[n, 0], flux[n, 1]
+        out = one + two - pltpu.roll(two, 1, 1)
+        out += pltpu.roll(row_0 * two - one, 1, 0)
+        out += row_2 * pltpu.roll(two - last_sub * one, 7, 0)
+        out += jnp.where(sub == 1, pltpu.roll(one, 6, 0), jnp.where(sub == 2, pltpu.roll(one, 3, 0), 0.0))
+        out -= jnp.where(sub == 5, pltpu.roll(one, 2, 0), 0.0)
+        img[n] = out
+        out = jnp.where(valid, out, 0.0)
+        v = jnp.where(valid, v, 0.0)
+        return norm + v * v, curve + v * out, energy + out * out
+
+    def eight_far_modes(h, sums):
         for j in range(8):
-            n = 8 * h + j
-            o, i = 4 * h + j // 2, j % 2
+            n = 16 + 8 * h + j
+            o, i = 8 + 4 * h + j // 2, j % 2
             one = aa[0, 0] * ff[16 * i + o, 0]
             two = aa[0, 1] * ff[16 * i + o, 1]
             for e in range(TERMS):
@@ -244,27 +262,8 @@
                 two += w * (aa[k, 1] * ff[p, 1])
             flux[n, 0] = one
             flux[n, 1] = two
-        return carry
-
-    row_0 = jnp.where(row == 0, 1.0, 0.0).astype(F32)
-    row_2 = jnp.where(row == 2, 1.0, 0.0).astype(F32)
-    last_sub = jnp.where(sub == 7, 1.0, 0.0).astype(F32)
-
-    def sixteen_modes(h, carry):
-        norm, curve, energy = carry
-        for j in range(16):
-            n = 16 * h + j
-            one, two = flux[n, 0], flux[n, 1]
-            out = one + two - pltpu.roll(two, 1, 1)
-            out += pltpu.roll(row_0 * two - one, 1, 0)
-            out += row_2 * pltpu.roll(two - last_sub * one, 7, 0)
-            out += jnp.where(sub == 1, pltpu.roll(one, 6, 0), jnp.where(sub == 2, pltpu.roll(one, 3, 0), 0.0))
-            out -= jnp.where(sub == 5, pltpu.roll(one, 2, 0), 0.0)
-            img[n] = out
-            out = jnp.where(valid, out, 0.0)
-            v = jnp.where(valid, got[8 * h + j // 2, j % 2], 0.0)
-            norm, curve, energy = norm + v * v, curve + v * out, energy + out * out
-        return norm, curve, energy
+            sums = finish(n - 16, got[o - 8, i], sums)
+        return sums
 
     own_sum = xl * 8 + r
 
@@ -350,27 +349,17 @@
         @pl.when(get_edge)
         def _():
             all_of(got_edges, 16, edge_ss.at[0], edge_rs).wait_recv()
-
-        @pl.when(get_low)
-        def _():
             for i in range(2):
-                for z in range(2):
-                    at = (pl.ds(16 * i, 16), 0, slice(4 * z, 4 * z + 1))
-                    ff[at] = ff[at] + got_edges[:, 2 * i + z : 2 * i + z + 1, :]
-
-        @pl.when(get_high)
-        def _():
-            for i in range(2):
-                for z in range(2):
-                    at = (pl.ds(16 * i, 16), 0, slice(4 * z + 2, 4 * z + 3))
-                    ff[at] = ff[at] - got_edges[:, 2 * i + z : 2 * i + z + 1, :]
+                for d in range(16):
+                    ff[16 * i + d, 0] = ff[16 * i + d, 0] + got_edges[d, i]
 
         zero = jnp.zeros((8, 128), F32)
         lax.fori_loop(0, 2, eight_modes, 0)
         for copy in far:
             copy.wait()
-        lax.fori_loop(2, 4, eight_far_modes, 0)
-        parts = lax.fori_loop(0, 2, sixteen_modes, (zero, zero, zero))
+        parts = lax.fori_loop(0, 2, eight_far_modes, (zero, zero, zero))
+        for n in range(16, MODES):
+            parts = finish(n, got[n // 2, n % 2], parts)
 
         sum_a[...] = jnp.zeros((4, 128), F32)
         for i in range(3):
@@ -497,12 +486,12 @@
             pltpu.VMEM((2, TERMS), i32),
             pltpu.VMEM((2, TERMS), F32),
             pltpu.VMEM((8, 2, 8, 128), F32),
-            pltpu.VMEM((2, 4, 128), F32),
+            pltpu.VMEM((2, 2, 8, 128), F32),
             pltpu.VMEM((KL, 2, 128), F32),
             pltpu.VMEM((2, 2, 128), i32),
             pltpu.VMEM((2, 128), F32),
             pltpu.VMEM((16, 2, 8, 128), F32),
-            pltpu.VMEM((16, 4, 128), F32),
+            pltpu.VMEM((16, 2, 8, 128), F32),
             pltpu.VMEM((KL, 2, 128), F32),
             pltpu.VMEM((16, 2, 2, 128), i32),
             pltpu.VMEM((16, 2, 128), F32),

time: 33.9 us -> 33.8 us (level)
  no operation moved by 1% of the time
where the time goes in v6:
time: 33.8 us; the launch traced here: 33.7 us
  Pallas kernels  33.1 us (98%)
  between operations  0.64 us (2%)
    pallas_call x1, Pallas kernels, on_device(): pl.pallas_call(galerkin, out_shape=(field,) * 4, in_specs=[anywhere] * 6,...  32.4 us
    pallas_call x1, Pallas kernels, on_device(): pl.pallas_call(deliver, out_shape=(jax.ShapeDtypeStruct(residual.shape, F...  0.69 us

profile of v6, /device:TPU:1, one launch (start us, length us, event | category | flops | bytes accessed | tf_op | source)
XLA Modules:
  0.0 33.7 jit_solution(14954793794403874042)
XLA Ops:
  0.6 32.4 %galerkin.1 = (f32[2,2,16,128]{3,2,1,0:T(8,128)S(1)}, f32[2,2,16,128]{3,2,1,0:T(8,128)S(1)}, f32[2,2,16,128]{3,2,1,0:T(8,128)S(1)}, f32[2,2,16,128]{3,2,1,0:T(8,128)S(1)}) custom-call(f32[2,2,16,128]{3,2,1,0:T(8,128)} %res_hbm.1, f32[2,2,16,128]{3,2,1,0:T(8,128)} %sol_hbm.1, f32[21,2,16,128]{3,2,1,0:T(8,128)} %kl_hbm.1, s32[2,24]{1,0:T(2,128)} %part_hbm.1, ...), custom_call_target="tpu_custom_call" | custom-call | tf_op jit(solution)/shard_map/galerkin/pallas_call | solution.py:476
  33.0 0.7 %deliver.1 = (f32[2,2,16,128]{3,2,1,0:T(8,128)}, f32[2,2,16,128]{3,2,1,0:T(8,128)}, f32[2,2,16,128]{3,2,1,0:T(8,128)}, f32[2,2,16,128]{3,2,1,0:T(8,128)}) custom-call(f32[2,2,16,128]{3,2,1,0:T(8,128)S(1)} %get-tuple-element.8.refs_0_, f32[2,2,16,128]{3,2,1,0:T(8,128)S(1)} %get-tuple-element.9.refs_1_, f32[2,2,16,128]{3,2,1,0:T(8,128)S(1)} %get-tuple-element.10.refs_2_, ...), custom_call_target="tpu_custom_call" | custom-call | tf_op jit(solution)/shard_map/deliver/pallas_call | solution.py:529

commit v7 on v6

--- a/solution.py
+++ b/solution.py
@@ -104,9 +104,11 @@
     for load in loads[:4]:
         load.wait()
     p = part_v[...]
-    ints[0, :, 0:TERMS] = (p % 2) * 16 + (p // 8) % 2 * 8 + p // 16 * 4 + p // 2 % 4
-    ints[1, :, 0:TERMS] = term_v[...]
-    floats[:, 0:TERMS] = coef_v[...]
+    p = (p % 2) * 16 + (p // 8) % 2 * 8 + p // 16 * 4 + p // 2 % 4
+    for i in range(2):
+        ints[:, TERMS * i : TERMS * (i + 1)] = p[i : i + 1, :]
+        ints[:, TERMS * (i + 2) : TERMS * (i + 3)] = term_v[i : i + 1, :]
+        floats[:, TERMS * i : TERMS * (i + 1)] = coef_v[i : i + 1, :]
     for j in range(8):
         for i in range(2):
             for z in range(2):
@@ -211,8 +213,8 @@
     def weigh(h, carry):
         for i in range(2):
             for e in range(TERMS):
-                k = int_s[h, 1, i, e]
-                w = float_s[h, i, e]
+                k = int_s[h, 0, TERMS * (i + 2) + e]
+                w = float_s[h, 0, TERMS * i + e]
                 wa[2 * h + i, e, 0] = w * aa[k, 0]
                 wa[2 * h + i, e, 1] = w * aa[k, 1]
         return carry
@@ -224,7 +226,7 @@
             one = aa[0, 0] * ff[16 * i + o, 0]
             two = aa[0, 1] * ff[16 * i + o, 1]
             for e in range(TERMS):
-                p = int_s[o, 0, i, e]
+                p = int_s[o, 0, TERMS * i + e]
                 one += wa[n, e, 0] * ff[p, 0]
                 two += wa[n, e, 1] * ff[p, 1]
             flux[n, 0] = one
@@ -255,9 +257,9 @@
             one = aa[0, 0] * ff[16 * i + o, 0]
             two = aa[0, 1] * ff[16 * i + o, 1]
             for e in range(TERMS):
-                p = int_s[o, 0, i, e]
-                k = int_s[o, 1, i, e]
-                w = float_s[o, i, e]
+                p = int_s[o, 0, TERMS * i + e]
+                k = int_s[o, 0, TERMS * (i + 2) + e]
+                w = float_s[o, 0, TERMS * i + e]
                 one += w * (aa[k, 0] * ff[p, 0])
                 two += w * (aa[k, 1] * ff[p, 1])
             flux[n, 0] = one
@@ -488,15 +490,15 @@
             pltpu.VMEM((8, 2, 8, 128), F32),
             pltpu.VMEM((2, 2, 8, 128), F32),
             pltpu.VMEM((KL, 2, 128), F32),
-            pltpu.VMEM((2, 2, 128), i32),
-            pltpu.VMEM((2, 128), F32),
+            pltpu.VMEM((1, 128), i32),
+            pltpu.VMEM((1, 128), F32),
             pltpu.VMEM((16, 2, 8, 128), F32),
             pltpu.VMEM((16, 2, 8, 128), F32),
             pltpu.VMEM((KL, 2, 128), F32),
-            pltpu.VMEM((16, 2, 2, 128), i32),
-            pltpu.VMEM((16, 2, 128), F32),
-            pltpu.SMEM((16, 2, 2, 128), i32),
-            pltpu.SMEM((16, 2, 128), F32),
+            pltpu.VMEM((16, 1, 128), i32),
+            pltpu.VMEM((16, 1, 128), F32),
+            pltpu.SMEM((16, 1, 128), i32),
+            pltpu.SMEM((16, 1, 128), F32),
             pltpu.VMEM((KL, 8, 128), F32),
             pltpu.VMEM((KL, 2, 8, 128), F32),
             pltpu.VMEM((MODES // 2, TERMS, 2, 8, 128), F32),

time: 33.8 us -> 33.4 us (0.988)
  Pallas kernels: 33.1 us -> 32.6 us
    pallas_call x1, Pallas kernels: 32.4 us -> 31.9 us  [on_device(): pl.pallas_call(galerkin, out_shape=(field,) * 4, in_specs=[anywhere] * 6,...]
where the time goes in v7:
time: 33.4 us; the launch traced here: 33.2 us
  Pallas kernels  32.6 us (98%)
  between operations  0.64 us (2%)
    pallas_call x1, Pallas kernels, on_device(): pl.pallas_call(galerkin, out_shape=(field,) * 4, in_specs=[anywhere] * 6,...  31.9 us
    pallas_call x1, Pallas kernels, on_device(): pl.pallas_call(deliver, out_shape=(jax.ShapeDtypeStruct(residual.shape, F...  0.69 us

profile of v7, /device:TPU:1, one launch (start us, length us, event | category | flops | bytes accessed | tf_op | source)
XLA Modules:
  0.0 33.2 jit_solution(14219229690191722693)
XLA Ops:
  0.6 31.9 %galerkin.1 = (f32[2,2,16,128]{3,2,1,0:T(8,128)S(1)}, f32[2,2,16,128]{3,2,1,0:T(8,128)S(1)}, f32[2,2,16,128]{3,2,1,0:T(8,128)S(1)}, f32[2,2,16,128]{3,2,1,0:T(8,128)S(1)}) custom-call(f32[2,2,16,128]{3,2,1,0:T(8,128)} %res_hbm.1, f32[2,2,16,128]{3,2,1,0:T(8,128)} %sol_hbm.1, f32[21,2,16,128]{3,2,1,0:T(8,128)} %kl_hbm.1, s32[2,24]{1,0:T(2,128)} %part_hbm.1, ...), custom_call_target="tpu_custom_call" | custom-call | tf_op jit(solution)/shard_map/galerkin/pallas_call | solution.py:478
  32.5 0.7 %deliver.1 = (f32[2,2,16,128]{3,2,1,0:T(8,128)}, f32[2,2,16,128]{3,2,1,0:T(8,128)}, f32[2,2,16,128]{3,2,1,0:T(8,128)}, f32[2,2,16,128]{3,2,1,0:T(8,128)}) custom-call(f32[2,2,16,128]{3,2,1,0:T(8,128)S(1)} %get-tuple-element.8.refs_0_, f32[2,2,16,128]{3,2,1,0:T(8,128)S(1)} %get-tuple-element.9.refs_1_, f32[2,2,16,128]{3,2,1,0:T(8,128)S(1)} %get-tuple-element.10.refs_2_, ...), custom_call_target="tpu_custom_call" | custom-call | tf_op jit(solution)/shard_map/deliver/pallas_call | solution.py:531

commit v8 on v7

--- a/solution.py
+++ b/solution.py
@@ -163,13 +163,17 @@
     for i in range(7):
         int_copy(i).start()
         float_copy(i).start()
+
+    @pl.when(sends)
+    def _():
+        int_copy(7).start()
+        float_copy(7).start()
+
     for i in range(7):
         main_copy(i).start()
 
     @pl.when(sends)
     def _():
-        int_copy(7).start()
-        float_copy(7).start()
         main_copy(7).start()
 
     tell(0)

time: 33.4 us -> 33.4 us (level)
  no operation moved by 1% of the time
where the time goes in v8:
time: 33.4 us; the launch traced here: 33.2 us
  Pallas kernels  32.6 us (98%)
  between operations  0.64 us (2%)
    pallas_call x1, Pallas kernels, on_device(): pl.pallas_call(galerkin, out_shape=(field,) * 4, in_specs=[anywhere] * 6,...  31.9 us
    pallas_call x1, Pallas kernels, on_device(): pl.pallas_call(deliver, out_shape=(jax.ShapeDtypeStruct(residual.shape, F...  0.69 us

profile of v8, /device:TPU:1, one launch (start us, length us, event | category | flops | bytes accessed | tf_op | source)
XLA Modules:
  0.0 33.2 jit_solution(12118926226497361609)
XLA Ops:
  0.6 31.9 %galerkin.1 = (f32[2,2,16,128]{3,2,1,0:T(8,128)S(1)}, f32[2,2,16,128]{3,2,1,0:T(8,128)S(1)}, f32[2,2,16,128]{3,2,1,0:T(8,128)S(1)}, f32[2,2,16,128]{3,2,1,0:T(8,128)S(1)}) custom-call(f32[2,2,16,128]{3,2,1,0:T(8,128)} %res_hbm.1, f32[2,2,16,128]{3,2,1,0:T(8,128)} %sol_hbm.1, f32[21,2,16,128]{3,2,1,0:T(8,128)} %kl_hbm.1, s32[2,24]{1,0:T(2,128)} %part_hbm.1, ...), custom_call_target="tpu_custom_call" | custom-call | tf_op jit(solution)/shard_map/galerkin/pallas_call | solution.py:482
  32.5 0.7 %deliver.1 = (f32[2,2,16,128]{3,2,1,0:T(8,128)}, f32[2,2,16,128]{3,2,1,0:T(8,128)}, f32[2,2,16,128]{3,2,1,0:T(8,128)}, f32[2,2,16,128]{3,2,1,0:T(8,128)}) custom-call(f32[2,2,16,128]{3,2,1,0:T(8,128)S(1)} %get-tuple-element.8.refs_0_, f32[2,2,16,128]{3,2,1,0:T(8,128)S(1)} %get-tuple-element.9.refs_1_, f32[2,2,16,128]{3,2,1,0:T(8,128)S(1)} %get-tuple-element.10.refs_2_, ...), custom_call_target="tpu_custom_call" | custom-call | tf_op jit(solution)/shard_map/deliver/pallas_call | solution.py:535
